TPU v7x, 32 devices: a whole 2x2x4 slice. The times are simulated.
32 devices in a mesh: row: 4 (over y, x), col: 4 (over z), layer: 2 (over core).
Axes of the slice: x: 2, y: 2, z: 4, core: 2. Of those that a mesh axis runs over, the one named last changes fastest.
Arguments:
- density: bfloat16 [1024, 1024], P('row', 'col'), may hold values from -0.25 to 0.25
- panel: bfloat16 [1024, 8192], P('row', 'col'), may hold values from -6 to 6
- pattern: int32 [8, 8], P('row', 'col'), may hold values 0 or 1
Outputs:
- purified: bfloat16 [1024, 8192], P('row', ('col', 'layer'))
All inputs are finite; a program needn't handle non-finite values. No bound on the sum of `pattern` on one device may be relied on, other than what follows from the above.
Results may differ from a plain program's by a relative error of at most 0.0034.
Values may be sent and summed in bfloat16 or wider, within the bound.
A program may use at most 64 MiB of HBM per device.

v0:
```python
import jax
import jax.numpy as jnp
from jax import lax
from jax.sharding import PartitionSpec as P

BS = 128


def passed_along(block, axis, distance):
    devices = range(lax.axis_size(axis))
    route = [((i - distance) % len(devices), i) for i in devices]
    return lax.ppermute(block, axis, route)


def multiply(left_tile, right_tile, step_count, offset, left_shift, right_shift):
    row_count = lax.axis_size("row")
    col_count = lax.axis_size("col")
    group_size = row_count // col_count
    row_index = lax.axis_index("row")
    col_index = lax.axis_index("col")
    slice_width = left_tile.shape[1] // group_size
    left_amount = (row_index + offset) // group_size % col_count
    right_amount = (group_size * col_index + offset) % row_count
    for bit_number in range((col_count - 1).bit_length()):
        shifted = left_shift(left_tile, col_count - (1 << bit_number))
        left_tile = jnp.where(left_amount // (1 << bit_number) % 2 == 1, shifted, left_tile)
    for bit_number in range((row_count - 1).bit_length()):
        shifted = right_shift(right_tile, row_count - (1 << bit_number))
        right_tile = jnp.where(right_amount // (1 << bit_number) % 2 == 1, shifted, right_tile)
    running = jnp.zeros((left_tile.shape[0], right_tile.shape[1]), jnp.float32)
    for segment in range(step_count):
        position = (row_index + offset + segment) % group_size
        section = lax.dynamic_slice_in_dim(left_tile, position * slice_width, slice_width, 1)
        running = running + jnp.dot(section, right_tile, preferred_element_type=jnp.float32)
        if segment + 1 < step_count:
            right_tile = right_shift(right_tile, row_count - 1)
            shifted = left_shift(left_tile, col_count - 1)
            left_tile = jnp.where(
                (row_index + offset + segment + 1) % group_size == 0, shifted, left_tile
            )
    return running


def shards(density, panel, pattern):
    row_count = lax.axis_size("row")
    layer_count = lax.axis_size("layer")
    layer_index = lax.axis_index("layer")
    mask_rows, mask_cols = pattern.shape
    tile_rows, tile_inner = density.shape
    block_mask = pattern.astype(jnp.bfloat16)
    filtered = (
        density.reshape(mask_rows, BS, mask_cols, BS) * block_mask[:, None, :, None]
    ).reshape(tile_rows, tile_inner)
    quarter = panel.shape[1] // layer_count

    def move_left(tile_data, amount):
        return passed_along(tile_data, "col", amount)

    def move_right(tile_data, amount):
        return passed_along(tile_data, "row", amount)

    layer_depth = row_count // layer_count
    offset = layer_index * layer_depth
    partial_value = multiply(filtered, panel, layer_depth, offset, move_left, move_right)
    square = lax.psum(partial_value, "layer")
    partial_cubic = multiply(
        filtered, square.astype(jnp.bfloat16), layer_depth, offset, move_left, move_right
    )
    cubic = lax.psum_scatter(partial_cubic, "layer", scatter_dimension=1, tiled=True)
    squares_kept = lax.dynamic_slice_in_dim(square, layer_index * quarter, quarter, 1)
    return (3.0 * squares_kept - 2.0 * cubic).astype(jnp.bfloat16)


def solution(mesh):
    in_specs = (P("row", "col"), P("row", "col"), P("row", "col"))
    out_specs = P("row", ("col", "layer"))
    return jax.shard_map(shards, mesh=mesh, in_specs=in_specs, out_specs=out_specs, check_vma=False)
```

profile of v0, /device:TPU:0, one launch (start us, length us, event | category | flops | bytes accessed | tf_op | source)
XLA Modules:
  0.0 207.4 jit_solution(7336617560087688754)
XLA Ops:
  6.5 3.9 %collective-permute-start.2 = (bf16[256,2048]{1,0:T(8,128)(2,1)}, bf16[256,2048]{1,0:T(8,128)(2,1)S(1)}, u32[]{:S(2)}, u32[]{:S(2)}) collective-permute-start(bf16[256,2048]{1,0:T(8,128)(2,1)} %param.4), channel_id=1, source_target_pairs={{8,0},{16,8},{24,16},{0,24},{9,1},{17,9},{25,17},{1,25},{10,2},{18... | collective-permute-start | bytes 3145736 | tf_op jit(solution)/shard_map/ppermute | solution.py:12
  10.4 22.7 %collective-permute-done.2 = bf16[256,2048]{1,0:T(8,128)(2,1)S(1)} collective-permute-done((bf16[256,2048]{1,0:T(8,128)(2,1)}, bf16[256,2048]{1,0:T(8,128)(2,1)S(1)}, u32[]{:S(2)}, u32[]{:S(2)}) %collective-permute-start.2) | collective-permute-done | bytes 1048608 | tf_op jit(solution)/shard_map/ppermute | solution.py:12
  34.5 1.5 collective-permute-start.3
  36.0 22.6 %collective-permute-done.3 = bf16[256,2048]{1,0:T(8,128)(2,1)S(1)} collective-permute-done((bf16[256,2048]{1,0:T(8,128)(2,1)S(1)}, bf16[256,2048]{1,0:T(8,128)(2,1)S(1)}, u32[]{:S(2)}, u32[]{:S(2)}) %collective-permute-start.3) | collective-permute-done | bytes 1048608 | tf_op jit(solution)/shard_map/ppermute | solution.py:12
  58.7 3.3 %collective-permute-start.5 = (bf16[256,2048]{1,0:T(8,128)(2,1)S(1)}, bf16[256,2048]{1,0:T(8,128)(2,1)S(1)}, u32[]{:S(2)}, u32[]{:S(2)}) collective-permute-start(bf16[256,2048]{1,0:T(8,128)(2,1)S(1)} %broadcast_select_fusion.3), channel_id=1, source_target_pairs={{8,0},{16,8},{24,16},{0,24},{9,1},{17,9},{25,17},{1,25},{10,2},{18... | collective-permute-start | bytes 3145736 | tf_op jit(solution)/shard_map/ppermute | solution.py:12
  62.2 2.4 %collective-permute-start = (bf16[256,256]{1,0:T(8,128)(2,1)S(1)}, bf16[256,256]{1,0:T(8,128)(2,1)S(1)}, u32[]{:S(2)}, u32[]{:S(2)}) collective-permute-start(bf16[256,256]{1,0:T(8,128)(2,1)S(1)} %bitcast_multiply_fusion), channel_id=1, source_target_pairs={{2,0},{4,2},{6,4},{0,6},{3,1},{5,3},{7,5},{1,7},{10,8},{12,10},{14... | collective-permute-start | bytes 393224 | tf_op jit(solution)/shard_map/ppermute | solution.py:12
  64.7 2.7 %collective-permute-done = bf16[256,256]{1,0:T(8,128)(2,1)S(1)} collective-permute-done((bf16[256,256]{1,0:T(8,128)(2,1)S(1)}, bf16[256,256]{1,0:T(8,128)(2,1)S(1)}, u32[]{:S(2)}, u32[]{:S(2)}) %collective-permute-start) | collective-permute-done | bytes 131104 | tf_op jit(solution)/shard_map/ppermute | solution.py:12
  67.3 2.9 %collective-permute-start.1 = (bf16[256,256]{1,0:T(8,128)(2,1)S(1)}, bf16[256,256]{1,0:T(8,128)(2,1)S(1)}, u32[]{:S(2)}, u32[]{:S(2)}) collective-permute-start(bf16[256,256]{1,0:T(8,128)(2,1)S(1)} %broadcast_select_fusion.4), channel_id=1, source_target_pairs={{4,0},{6,2},{0,4},{2,6},{5,1},{7,3},{1,5},{3,7},{12,8},{14,10},{8,... | collective-permute-start | bytes 393224 | tf_op jit(solution)/shard_map/ppermute | solution.py:12
  70.2 3.2 %collective-permute-done.1 = bf16[256,256]{1,0:T(8,128)(2,1)S(1)} collective-permute-done((bf16[256,256]{1,0:T(8,128)(2,1)S(1)}, bf16[256,256]{1,0:T(8,128)(2,1)S(1)}, u32[]{:S(2)}, u32[]{:S(2)}) %collective-permute-start.1) | collective-permute-done | bytes 131104 | tf_op jit(solution)/shard_map/ppermute | solution.py:12
  73.4 5.1 %collective-permute-start.4 = (bf16[256,256]{1,0:T(8,128)(2,1)S(1)}, bf16[256,256]{1,0:T(8,128)(2,1)S(1)}, u32[]{:S(2)}, u32[]{:S(2)}) collective-permute-start(bf16[256,256]{1,0:T(8,128)(2,1)S(1)} %broadcast_select_fusion.5), channel_id=1, source_target_pairs={{2,0},{4,2},{6,4},{0,6},{3,1},{5,3},{7,5},{1,7},{10,8},{12,10},{14... | collective-permute-start | bytes 393224 | tf_op jit(solution)/shard_map/ppermute | solution.py:12
  78.5 2.5 %collective-permute-done.4 = bf16[256,256]{1,0:T(8,128)(2,1)S(1)} collective-permute-done((bf16[256,256]{1,0:T(8,128)(2,1)S(1)}, bf16[256,256]{1,0:T(8,128)(2,1)S(1)}, u32[]{:S(2)}, u32[]{:S(2)}) %collective-permute-start.4) | collective-permute-done | bytes 131104 | tf_op jit(solution)/shard_map/ppermute | solution.py:12
  81.0 1.7 collective-permute-done.5
  83.1 1.8 convolution_add_fusion.1
  85.0 22.5 %all-reduce.2.cloned.1.call-done = f32[256,2048]{1,0:T(8,128)} async-done(((f32[256,2048]{1,0:T(8,128)}), f32[256,2048]{1,0:T(8,128)}) %all-reduce.2.cloned.1.call-update) | async-done | bytes 2097168 | tf_op jit(solution)/shard_map/psum | solution.py:65
  107.4 1.9 convert_element_type.10
  109.3 2.7 %collective-permute-start.6 = (bf16[256,2048]{1,0:T(8,128)(2,1)S(1)}, bf16[256,2048]{1,0:T(8,128)(2,1)S(1)}, u32[]{:S(2)}, u32[]{:S(2)}) collective-permute-start(bf16[256,2048]{1,0:T(8,128)(2,1)S(1)} %convert_element_type.10), channel_id=1, source_target_pairs={{8,0},{16,8},{24,16},{0,24},{9,1},{17,9},{25,17},{1,25},{10,2},{18... | collective-permute-start | bytes 3145736 | tf_op jit(solution)/shard_map/ppermute | solution.py:12
  112.0 22.9 %collective-permute-done.6 = bf16[256,2048]{1,0:T(8,128)(2,1)S(1)} collective-permute-done((bf16[256,2048]{1,0:T(8,128)(2,1)S(1)}, bf16[256,2048]{1,0:T(8,128)(2,1)S(1)}, u32[]{:S(2)}, u32[]{:S(2)}) %collective-permute-start.6) | collective-permute-done | bytes 1048608 | tf_op jit(solution)/shard_map/ppermute | solution.py:12
  135.1 1.6 collective-permute-start.7
  136.8 23.0 %collective-permute-done.7 = bf16[256,2048]{1,0:T(8,128)(2,1)S(1)} collective-permute-done((bf16[256,2048]{1,0:T(8,128)(2,1)S(1)}, bf16[256,2048]{1,0:T(8,128)(2,1)S(1)}, u32[]{:S(2)}, u32[]{:S(2)}) %collective-permute-start.7) | collective-permute-done | bytes 1048608 | tf_op jit(solution)/shard_map/ppermute | solution.py:12
  159.9 3.4 %collective-permute-start.8 = (bf16[256,2048]{1,0:T(8,128)(2,1)S(1)}, bf16[256,2048]{1,0:T(8,128)(2,1)S(1)}, u32[]{:S(2)}, u32[]{:S(2)}) collective-permute-start(bf16[256,2048]{1,0:T(8,128)(2,1)S(1)} %broadcast_select_fusion.2), channel_id=1, source_target_pairs={{8,0},{16,8},{24,16},{0,24},{9,1},{17,9},{25,17},{1,25},{10,2},{18... | collective-permute-start | bytes 3145736 | tf_op jit(solution)/shard_map/ppermute | solution.py:12
  163.3 21.1 %collective-permute-done.8 = bf16[256,2048]{1,0:T(8,128)(2,1)S(1)} collective-permute-done((bf16[256,2048]{1,0:T(8,128)(2,1)S(1)}, bf16[256,2048]{1,0:T(8,128)(2,1)S(1)}, u32[]{:S(2)}, u32[]{:S(2)}) %collective-permute-start.8) | collective-permute-done | bytes 1048608 | tf_op jit(solution)/shard_map/ppermute | solution.py:12
  184.9 1.8 convolution_add_fusion
  186.7 11.7 %reduce-scatter.2.cloned.1.call-done = f32[256,1024]{1,0:T(8,128)} async-done(((f32[256,2048]{1,0:T(8,128)}), f32[256,1024]{1,0:T(8,128)}) %reduce-scatter.2.cloned.1.call-update) | async-done | bytes 1048592 | tf_op jit(solution)/shard_map/reduce_scatter | solution.py:69
  198.4 2.2 %subtract_convert_fusion = bf16[256,1024]{1,0:T(8,128)(2,1)} fusion(f32[256,1024]{1,0:T(8,128)} %reduce-scatter.2.cloned.1.call-done, f32[256,2048]{1,0:T(8,128)S(1)} %copy-done, s32[]{:T(128)S(6)} %select_n.133), kind=kLoop, calls=%fused_computation.2 | loop fusion | flops 1048576 | bytes 2621444 | tf_op jit(solution)/shard_map/convert_element_type | solution.py:71
  (21 shorter events, 2.9 us)
Async XLA Ops:
  6.5 29.5 %copy-start.2 = (s32[2,2]{1,0:T(2,128)S(1)}, s32[2,2]{1,0:T(2,128)}, u32[]{:S(2)}) copy-start(s32[2,2]{1,0:T(2,128)} %param.5) | copy-start | bytes 52
  6.5 100.9 %all-reduce.2.cloned.1.call-start = ((), (), s32[]{:S(2)}) async-start(), calls=%async_computation.1 | async-start | bytes 4194304 | tf_op jit(solution)/shard_map/psum | solution.py:65
  6.5 26.6 %collective-permute-start.2 = (bf16[256,2048]{1,0:T(8,128)(2,1)}, bf16[256,2048]{1,0:T(8,128)(2,1)S(1)}, u32[]{:S(2)}, u32[]{:S(2)}) collective-permute-start(bf16[256,2048]{1,0:T(8,128)(2,1)} %param.4), channel_id=1, source_target_pairs={{8,0},{16,8},{24,16},{0,24},{9,1},{17,9},{25,17},{1,25},{10,2},{18... | collective-permute-start | bytes 3145736 | tf_op jit(solution)/shard_map/ppermute | solution.py:12
  34.5 27.7 %copy-start.1 = (bf16[256,256]{1,0:T(8,128)(2,1)S(1)}, bf16[256,256]{1,0:T(8,128)(2,1)}, u32[]{:S(2)}) copy-start(bf16[256,256]{1,0:T(8,128)(2,1)} %param.3) | copy-start | bytes 393220
  34.5 24.1 %collective-permute-start.3 = (bf16[256,2048]{1,0:T(8,128)(2,1)S(1)}, bf16[256,2048]{1,0:T(8,128)(2,1)S(1)}, u32[]{:S(2)}, u32[]{:S(2)}) collective-permute-start(bf16[256,2048]{1,0:T(8,128)(2,1)S(1)} %broadcast_select_fusion.1), channel_id=1, source_target_pairs={{16,0},{24,8},{0,16},{8,24},{17,1},{25,9},{1,17},{9,25},{18,2},{26... | collective-permute-start | bytes 3145736 | tf_op jit(solution)/shard_map/ppermute | solution.py:12
  58.7 24.0 %collective-permute-start.5 = (bf16[256,2048]{1,0:T(8,128)(2,1)S(1)}, bf16[256,2048]{1,0:T(8,128)(2,1)S(1)}, u32[]{:S(2)}, u32[]{:S(2)}) collective-permute-start(bf16[256,2048]{1,0:T(8,128)(2,1)S(1)} %broadcast_select_fusion.3), channel_id=1, source_target_pairs={{8,0},{16,8},{24,16},{0,24},{9,1},{17,9},{25,17},{1,25},{10,2},{18... | collective-permute-start | bytes 3145736 | tf_op jit(solution)/shard_map/ppermute | solution.py:12
  62.2 5.1 %collective-permute-start = (bf16[256,256]{1,0:T(8,128)(2,1)S(1)}, bf16[256,256]{1,0:T(8,128)(2,1)S(1)}, u32[]{:S(2)}, u32[]{:S(2)}) collective-permute-start(bf16[256,256]{1,0:T(8,128)(2,1)S(1)} %bitcast_multiply_fusion), channel_id=1, source_target_pairs={{2,0},{4,2},{6,4},{0,6},{3,1},{5,3},{7,5},{1,7},{10,8},{12,10},{14... | collective-permute-start | bytes 393224 | tf_op jit(solution)/shard_map/ppermute | solution.py:12
  67.3 6.0 %collective-permute-start.1 = (bf16[256,256]{1,0:T(8,128)(2,1)S(1)}, bf16[256,256]{1,0:T(8,128)(2,1)S(1)}, u32[]{:S(2)}, u32[]{:S(2)}) collective-permute-start(bf16[256,256]{1,0:T(8,128)(2,1)S(1)} %broadcast_select_fusion.4), channel_id=1, source_target_pairs={{4,0},{6,2},{0,4},{2,6},{5,1},{7,3},{1,5},{3,7},{12,8},{14,10},{8,... | collective-permute-start | bytes 393224 | tf_op jit(solution)/shard_map/ppermute | solution.py:12
  73.4 7.6 %collective-permute-start.4 = (bf16[256,256]{1,0:T(8,128)(2,1)S(1)}, bf16[256,256]{1,0:T(8,128)(2,1)S(1)}, u32[]{:S(2)}, u32[]{:S(2)}) collective-permute-start(bf16[256,256]{1,0:T(8,128)(2,1)S(1)} %broadcast_select_fusion.5), channel_id=1, source_target_pairs={{2,0},{4,2},{6,4},{0,6},{3,1},{5,3},{7,5},{1,7},{10,8},{12,10},{14... | collective-permute-start | bytes 393224 | tf_op jit(solution)/shard_map/ppermute | solution.py:12
  84.9 113.5 %reduce-scatter.2.cloned.1.call-start = ((), (), s32[]{:S(2)}) async-start(), calls=%async_computation.2 | async-start | bytes 3145728 | tf_op jit(solution)/shard_map/reduce_scatter | solution.py:69
  107.4 27.5 %copy-start = (f32[256,2048]{1,0:T(8,128)S(1)}, f32[256,2048]{1,0:T(8,128)}, u32[]{:S(2)}) copy-start(f32[256,2048]{1,0:T(8,128)} %all-reduce.2.cloned.1.call-done) | copy-start | bytes 6291460
  109.3 25.6 %collective-permute-start.6 = (bf16[256,2048]{1,0:T(8,128)(2,1)S(1)}, bf16[256,2048]{1,0:T(8,128)(2,1)S(1)}, u32[]{:S(2)}, u32[]{:S(2)}) collective-permute-start(bf16[256,2048]{1,0:T(8,128)(2,1)S(1)} %convert_element_type.10), channel_id=1, source_target_pairs={{8,0},{16,8},{24,16},{0,24},{9,1},{17,9},{25,17},{1,25},{10,2},{18... | collective-permute-start | bytes 3145736 | tf_op jit(solution)/shard_map/ppermute | solution.py:12
  135.1 24.6 %collective-permute-start.7 = (bf16[256,2048]{1,0:T(8,128)(2,1)S(1)}, bf16[256,2048]{1,0:T(8,128)(2,1)S(1)}, u32[]{:S(2)}, u32[]{:S(2)}) collective-permute-start(bf16[256,2048]{1,0:T(8,128)(2,1)S(1)} %broadcast_select_fusion), channel_id=1, source_target_pairs={{16,0},{24,8},{0,16},{8,24},{17,1},{25,9},{1,17},{9,25},{18,2},{26... | collective-permute-start | bytes 3145736 | tf_op jit(solution)/shard_map/ppermute | solution.py:12
  159.9 24.6 %collective-permute-start.8 = (bf16[256,2048]{1,0:T(8,128)(2,1)S(1)}, bf16[256,2048]{1,0:T(8,128)(2,1)S(1)}, u32[]{:S(2)}, u32[]{:S(2)}) collective-permute-start(bf16[256,2048]{1,0:T(8,128)(2,1)S(1)} %broadcast_select_fusion.2), channel_id=1, source_target_pairs={{8,0},{16,8},{24,16},{0,24},{9,1},{17,9},{25,17},{1,25},{10,2},{18... | collective-permute-start | bytes 3145736 | tf_op jit(solution)/shard_map/ppermute | solution.py:12
Sparse Core Ops, SparseCore 0:
  85.0 22.3 all-reduce.1
  186.8 11.5 reduce-scatter.1
where the time goes:
time: 208 us; the launch traced here: 207 us
  waiting for transfers between devices  157 us (75%)
  starting transfers between devices  26.9 us (13%)
  between operations  13.5 us (6%)
  other arithmetic  5.95 us (3%)
  matrix products  4.43 us (2%)
    ppermute x9, waiting for transfers between devices, passed_along(): return lax.ppermute(block, axis, route)  122 us
    ppermute x9, starting transfers between devices, passed_along(): return lax.ppermute(block, axis, route)  26.9 us
    psum x1, waiting for transfers between devices, shards(): square = lax.psum(partial_value, 'layer')  22.5 us
    reduce_scatter x1, waiting for transfers between devices, shards(): lax.psum_scatter(partial_cubic, 'layer', scatter_dimension=1, tiled=True)  11.7 us
    dot_general x4, matrix products, multiply(): jnp.dot(section, right_tile, preferred_element_type=jnp.float32)  4.43 us
  transfers between devices with their start and end apart: 11, of which 11 were waited for; matrix products, arithmetic and copies ran while one was open for 0% of the time, Pallas kernels for 0%

commit v1 on v0

v1 whole, which is shorter than its diff:
```python
import functools

import jax
import jax.numpy as jnp
from jax import lax
from jax.experimental import pallas as pl
from jax.experimental.pallas import tpu as pltpu
from jax.sharding import PartitionSpec as P

BS = 128
PIECES = 4
MESH = pl.DeviceIdType.MESH


def kernel(
    sizes, density_ref, panel_ref, pattern_ref, out_ref,
    tile, fcol, frow, grow, p, acc,
    load_sem, fc_s, fc_r, fr_s, fr_r, fs_s, fs_r, gr_s, gr_r, gs_s, gs_r,
    px_s, px_r, py_s, py_r, fx_s, fx_r, fy_s, fy_r,
):
    R, A, C = sizes
    B = R // A
    tr, ti = density_ref.shape
    half = ti // 2
    W = p.shape[2]
    wq = W // PIECES
    r = lax.axis_index("row")
    c = lax.axis_index("col")
    l = lax.axis_index("layer")
    x = lax.rem(r, A)
    y = r // A
    sib = 1 - l

    def rem_copy(ref, ssem, rsem, dev):
        return pltpu.make_async_remote_copy(
            src_ref=ref, dst_ref=ref, send_sem=ssem, recv_sem=rsem,
            device_id=dev, device_id_type=MESH,
        )

    barrier = pltpu.get_barrier_semaphore()
    for d in range(1, R):
        pl.semaphore_signal(barrier, inc=1, device_id={"row": lax.rem(r + d, R)}, device_id_type=MESH)
    for d in range(1, C):
        pl.semaphore_signal(barrier, inc=1, device_id={"col": lax.rem(c + d, C)}, device_id_type=MESH)
    pl.semaphore_signal(barrier, inc=1, device_id={"layer": sib}, device_id_type=MESH)

    load_tile = pltpu.make_async_copy(density_ref, tile, load_sem.at[0])
    load_tile.start()
    own_cols = pl.ds(pl.multiple_of(l * W, W), W)
    load_panel = pltpu.make_async_copy(panel_ref.at[:, own_cols], p.at[r], load_sem.at[1])
    load_panel.start()
    load_tile.wait()

    for a in range(tr // BS):
        for b in range(ti // BS):
            keep = pattern_ref[a, b].astype(jnp.float32)
            block = tile[a * BS:(a + 1) * BS, b * BS:(b + 1) * BS].astype(jnp.float32) * keep
            at = pl.ds(pl.multiple_of(c * ti + b * BS, BS), BS)
            frow[a * BS:(a + 1) * BS, at] = block.astype(jnp.bfloat16)
    def cols_of(col, layer):
        return pl.ds(pl.multiple_of(col * ti + layer * half, half), half)
    def rows_of(row):
        return pl.ds(pl.multiple_of(row * tr, tr), tr)
    fcol[rows_of(r), :] = frow[:, cols_of(c, l)]

    pl.semaphore_wait(barrier, R - 1 + C - 1 + 1)

    sends = []

    def send(ref, ssem, rsem, dev):
        copy = rem_copy(ref, ssem, rsem, dev)
        copy.start()
        sends.append(copy)

    def arrived(ref, ssem, rsem, dev):
        rem_copy(ref, ssem, rsem, dev).wait_recv()

    for d in range(1, R):
        send(fcol.at[rows_of(r), :], fc_s.at[d], fc_r.at[d], {"row": lax.rem(r + d, R)})
    for d in range(1, C):
        send(frow.at[:, cols_of(c, l)], fr_s.at[d], fr_r.at[d], {"col": lax.rem(c + d, C)})
    load_panel.wait()
    first, second = range(PIECES // 2), range(PIECES // 2, PIECES)

    def piece(row, q):
        return p.at[row, :, q * wq:(q + 1) * wq]

    def x_peer(d):
        return y * A + lax.rem(x + d, A)

    def y_peer(d):
        return lax.rem(y + d, B) * A + x

    x_order = list(second) + list(first)
    y_order = list(first) + list(second)
    for qx, qy in zip(x_order, y_order):
        for d in range(1, A):
            send(piece(r, qx), px_s.at[d, qx], px_r.at[d, qx], {"row": x_peer(d)})
        for d in range(1, B):
            send(piece(r, qy), py_s.at[d, qy], py_r.at[d, qy], {"row": y_peer(d)})

    for d in range(1, C):
        from_c = lax.rem(c - d + C, C)
        ref = frow.at[:, cols_of(from_c, l)]
        arrived(ref, fr_s.at[d], fr_r.at[d], {"col": from_c})
        send(ref, fs_s.at[d], fs_r.at[d], {"layer": sib})
    for d in range(1, C):
        from_c = lax.rem(c - d + C, C)
        arrived(frow.at[:, cols_of(from_c, sib)], fs_s.at[d], fs_r.at[d], {"layer": sib})
    for d in range(1, R):
        from_r = lax.rem(r - d + R, R)
        arrived(fcol.at[rows_of(from_r), :], fc_s.at[d], fc_r.at[d], {"row": from_r})

    grow[:, cols_of(c, l)] = jnp.dot(
        frow[...], fcol[...], preferred_element_type=jnp.float32
    ).astype(jnp.bfloat16)
    for d in range(1, C):
        send(grow.at[:, cols_of(c, l)], gr_s.at[d], gr_r.at[d], {"col": lax.rem(c + d, C)})
    send(grow.at[:, cols_of(c, l)], gs_s.at[0], gs_r.at[0], {"layer": sib})

    for qf, qs in zip(first, second):
        for dy in range(1, B):
            row = lax.rem(y - dy + B, B) * A + x
            arrived(piece(row, qf), py_s.at[dy, qf], py_r.at[dy, qf], {"row": row})
            for dx in range(1, A):
                send(piece(row, qf), fx_s.at[dy, dx, qf], fx_r.at[dy, dx, qf], {"row": x_peer(dx)})
        for dx in range(1, A):
            row = y * A + lax.rem(x - dx + A, A)
            arrived(piece(row, qs), px_s.at[dx, qs], px_r.at[dx, qs], {"row": row})
            for dy in range(1, B):
                send(piece(row, qs), fy_s.at[dy, dx, qs], fy_r.at[dy, dx, qs], {"row": y_peer(dy)})

    for d in range(1, C):
        from_c = lax.rem(c - d + C, C)
        ref = grow.at[:, cols_of(from_c, l)]
        arrived(ref, gr_s.at[d], gr_r.at[d], {"col": from_c})
        send(ref, gs_s.at[d], gs_r.at[d], {"layer": sib})
    for d in range(C):
        from_c = lax.rem(c - d + C, C)
        arrived(grow.at[:, cols_of(from_c, sib)], gs_s.at[d], gs_r.at[d], {"layer": sib})

    def term(row, q):
        at = pl.ds(pl.multiple_of(row * tr, tr), tr)
        right = p[row, :, q * wq:(q + 1) * wq]
        by_f = jnp.dot(frow[:, at], right, preferred_element_type=jnp.float32)
        by_g = jnp.dot(grow[:, at], right, preferred_element_type=jnp.float32)
        return 3.0 * by_f - 2.0 * by_g

    def part(q):
        return slice(q * wq, (q + 1) * wq)

    for q in range(PIECES):
        acc[:, part(q)] = term(r, q)
    for dx in range(1, A):
        row = y * A + lax.rem(x - dx + A, A)
        for q in x_order:
            if q in first:
                arrived(piece(row, q), px_s.at[dx, q], px_r.at[dx, q], {"row": row})
            acc[:, part(q)] += term(row, q)
    for dy in range(1, B):
        row = lax.rem(y - dy + B, B) * A + x
        for q in y_order:
            if q in second:
                arrived(piece(row, q), py_s.at[dy, q], py_r.at[dy, q], {"row": row})
            acc[:, part(q)] += term(row, q)
    for qf, qs in zip(first, second):
        for q, s_sem, r_sem in ((qf, fx_s, fx_r), (qs, fy_s, fy_r)):
            for dy in range(1, B):
                for dx in range(1, A):
                    row = lax.rem(y - dy + B, B) * A + lax.rem(x - dx + A, A)
                    arrived(piece(row, q), s_sem.at[dy, dx, q], r_sem.at[dy, dx, q], {"row": row})
            total = acc[:, part(q)]
            for dy in range(1, B):
                for dx in range(1, A):
                    row = lax.rem(y - dy + B, B) * A + lax.rem(x - dx + A, A)
                    total = total + term(row, q)
            out_ref[:, part(q)] = total.astype(jnp.bfloat16)

    for copy in sends:
        copy.wait_send()


def shards(R, C, L, density, panel, pattern):
    A = 1
    while A * A < R:
        A *= 2
    B = R // A
    tr, ti = density.shape
    half = ti // L
    W = panel.shape[1] // L
    K = tr * R
    dma = pltpu.SemaphoreType.DMA
    any_spec = pl.BlockSpec(memory_space=pl.ANY)
    bf16 = jnp.bfloat16
    return pl.pallas_call(
        functools.partial(kernel, (R, A, C)),
        out_shape=jax.ShapeDtypeStruct((tr, W), bf16),
        in_specs=[any_spec, any_spec, pl.BlockSpec(memory_space=pltpu.SMEM)],
        out_specs=pl.BlockSpec(memory_space=pltpu.VMEM),
        scratch_shapes=[
            pltpu.VMEM((tr, ti), bf16),
            pltpu.VMEM((K, half), bf16),
            pltpu.VMEM((tr, K), bf16),
            pltpu.VMEM((tr, K), bf16),
            pltpu.VMEM((R, tr, W), bf16),
            pltpu.VMEM((tr, W), jnp.float32),
            dma((2,)),
            dma((R,)), dma((R,)),
            dma((C,)), dma((C,)), dma((C,)), dma((C,)),
            dma((C,)), dma((C,)), dma((C,)), dma((C,)),
            dma((A, PIECES)), dma((A, PIECES)),
            dma((B, PIECES)), dma((B, PIECES)),
            dma((B, A, PIECES)), dma((B, A, PIECES)),
            dma((B, A, PIECES)), dma((B, A, PIECES)),
        ],
        compiler_params=pltpu.CompilerParams(
            collective_id=0, has_side_effects=True, vmem_limit_bytes=56 * 1024 * 1024
        ),
    )(density, panel, pattern)


def solution(mesh):
    R, C, L = mesh.shape["row"], mesh.shape["col"], mesh.shape["layer"]
    in_specs = (P("row", "col"), P("row", "col"), P("row", "col"))
    out_specs = P("row", ("col", "layer"))
    return jax.shard_map(
        functools.partial(shards, R, C, L),
        mesh=mesh, in_specs=in_specs, out_specs=out_specs, check_vma=False,
    )
```

time: 208 us -> 32 us (0.15)
  waiting for transfers between devices: 157 us -> 0 us
  Pallas kernels: 0 us -> 29.9 us
  starting transfers between devices: 26.9 us -> 0 us
  between operations: 13.5 us -> 0.01 us
  other arithmetic: 5.95 us -> 0 us
  matrix products: 4.43 us -> 0 us
    ppermute x9 -> x0, waiting for transfers between devices: 122 us -> none  [passed_along(): return lax.ppermute(block, axis, route)]
    pallas_call x0 -> x1, Pallas kernels: none -> 29.9 us  [shards(): pl.pallas_call(functools.partial(kernel, (R, A, C)), out_shape=jax.ShapeD...]
    ppermute x9 -> x0, starting transfers between devices: 26.9 us -> none  [passed_along(): return lax.ppermute(block, axis, route)]
    psum x1 -> x0, waiting for transfers between devices: 22.5 us -> none  [shards(): square = lax.psum(partial_value, 'layer')]
    reduce_scatter x1 -> x0, waiting for transfers between devices: 11.7 us -> none  [shards(): lax.psum_scatter(partial_cubic, 'layer', scatter_dimension=1, tiled=True)]
    dot_general x4 -> x0, matrix products: 4.43 us -> none  [multiply(): jnp.dot(section, right_tile, preferred_element_type=jnp.float32)]
    convert_element_type x3 -> x0, other arithmetic: 4.11 us -> none  [the longest x1 2.22 us: shards(): return (3.0 * squares_kept - 2.0 * cubic).astype(jnp.bfloat16)]
  transfers between devices with their start and end apart: 11 -> 0, of which waited for: 11 -> 0; matrix products, arithmetic and copies ran while one was open for 0% -> 0% of each run, Pallas kernels for 0% -> 0%
where the time goes in v1:
time: 32 us; the launch traced here: 31.8 us
  Pallas kernels  29.9 us (93%)
  local copies, waits for them, and re-layouts  1.87 us (6%)
    pallas_call x1, Pallas kernels, shards(): pl.pallas_call(functools.partial(kernel, (R, A, C)), out_shape=jax.ShapeD...  29.9 us
    unnamed x1, local copies, waits for them, and re-layouts  1.87 us

profile of v1, /device:TPU:0, one launch (start us, length us, event | category | flops | bytes accessed | tf_op | source)
XLA Modules:
  0.0 31.8 jit_solution(10659018782782996727)
XLA Ops:
  0.0 29.9 %shard_map.37 = bf16[256,1024]{1,0:T(8,128)(2,1)} custom-call(bf16[256,256]{1,0:T(8,128)(2,1)} %density_ref.1, bf16[256,2048]{1,0:T(8,128)(2,1)} %panel_ref.1, s32[2,2]{1,0:T(2,128)} %pattern_ref.1), custom_call_target="tpu_custom_call" | custom-call | tf_op jit(solution)/shard_map/pallas_call | solution.py:195
  29.9 1.9 %copy.5 = bf16[256,1024]{1,0:T(8,128)(2,1)} copy(bf16[256,1024]{1,0:T(8,128)(2,1)} %shard_map.37) | data formatting | bytes 1048576

commit v2 on v1

--- a/solution.py
+++ b/solution.py
@@ -13,8 +13,8 @@
 
 
 def kernel(
-    sizes, density_ref, panel_ref, pattern_ref, out_ref,
-    tile, fcol, frow, grow, p, acc,
+    sizes, density_ref, panel_ref, pattern_hbm, out_ref,
+    pattern_ref, tile, fcol, frow, grow, p, acc,
     load_sem, fc_s, fc_r, fr_s, fr_r, fs_s, fs_r, gr_s, gr_r, gs_s, gs_r,
     px_s, px_r, py_s, py_r, fx_s, fx_r, fy_s, fy_r,
 ):
@@ -44,11 +44,14 @@
         pl.semaphore_signal(barrier, inc=1, device_id={"col": lax.rem(c + d, C)}, device_id_type=MESH)
     pl.semaphore_signal(barrier, inc=1, device_id={"layer": sib}, device_id_type=MESH)
 
+    load_pattern = pltpu.make_async_copy(pattern_hbm, pattern_ref, load_sem.at[2])
+    load_pattern.start()
     load_tile = pltpu.make_async_copy(density_ref, tile, load_sem.at[0])
     load_tile.start()
     own_cols = pl.ds(pl.multiple_of(l * W, W), W)
     load_panel = pltpu.make_async_copy(panel_ref.at[:, own_cols], p.at[r], load_sem.at[1])
     load_panel.start()
+    load_pattern.wait()
     load_tile.wait()
 
     for a in range(tr // BS):
@@ -118,6 +121,19 @@
         send(grow.at[:, cols_of(c, l)], gr_s.at[d], gr_r.at[d], {"col": lax.rem(c + d, C)})
     send(grow.at[:, cols_of(c, l)], gs_s.at[0], gs_r.at[0], {"layer": sib})
 
+    def part(q):
+        return slice(q * wq, (q + 1) * wq)
+
+    def by(left, row, q):
+        at = pl.ds(pl.multiple_of(row * tr, tr), tr)
+        return jnp.dot(left[:, at], p[row, :, part(q)], preferred_element_type=jnp.float32)
+
+    def term(row, q):
+        return 3.0 * by(frow, row, q) - 2.0 * by(grow, row, q)
+
+    for q in range(PIECES):
+        acc[:, part(q)] = 3.0 * by(frow, r, q)
+
     for qf, qs in zip(first, second):
         for dy in range(1, B):
             row = lax.rem(y - dy + B, B) * A + x
@@ -139,18 +155,8 @@
         from_c = lax.rem(c - d + C, C)
         arrived(grow.at[:, cols_of(from_c, sib)], gs_s.at[d], gs_r.at[d], {"layer": sib})
 
-    def term(row, q):
-        at = pl.ds(pl.multiple_of(row * tr, tr), tr)
-        right = p[row, :, q * wq:(q + 1) * wq]
-        by_f = jnp.dot(frow[:, at], right, preferred_element_type=jnp.float32)
-        by_g = jnp.dot(grow[:, at], right, preferred_element_type=jnp.float32)
-        return 3.0 * by_f - 2.0 * by_g
-
-    def part(q):
-        return slice(q * wq, (q + 1) * wq)
-
     for q in range(PIECES):
-        acc[:, part(q)] = term(r, q)
+        acc[:, part(q)] -= 2.0 * by(grow, r, q)
     for dx in range(1, A):
         row = y * A + lax.rem(x - dx + A, A)
         for q in x_order:
@@ -194,17 +200,18 @@
     bf16 = jnp.bfloat16
     return pl.pallas_call(
         functools.partial(kernel, (R, A, C)),
-        out_shape=jax.ShapeDtypeStruct((tr, W), bf16),
-        in_specs=[any_spec, any_spec, pl.BlockSpec(memory_space=pltpu.SMEM)],
+        out_shape=pltpu.VMEM((tr, W), bf16),
+        in_specs=[any_spec] * 3,
         out_specs=pl.BlockSpec(memory_space=pltpu.VMEM),
         scratch_shapes=[
+            pltpu.SMEM(pattern.shape, jnp.int32),
             pltpu.VMEM((tr, ti), bf16),
             pltpu.VMEM((K, half), bf16),
             pltpu.VMEM((tr, K), bf16),
             pltpu.VMEM((tr, K), bf16),
             pltpu.VMEM((R, tr, W), bf16),
             pltpu.VMEM((tr, W), jnp.float32),
-            dma((2,)),
+            dma((3,)),
             dma((R,)), dma((R,)),
             dma((C,)), dma((C,)), dma((C,)), dma((C,)),
             dma((C,)), dma((C,)), dma((C,)), dma((C,)),

time: 32 us -> 29.3 us (0.916)
  Pallas kernels: 29.9 us -> 28.4 us
  local copies, waits for them, and re-layouts: 1.87 us -> 0.8 us
    pallas_call x1, Pallas kernels: 29.9 us -> 28.4 us  [shards(): pl.pallas_call(functools.partial(kernel, (R, A, C)), out_shape=pltpu.VMEM...]
    unnamed x1, local copies, waits for them, and re-layouts: 1.87 us -> 0.8 us
where the time goes in v2:
time: 29.3 us; the launch traced here: 29.2 us
  Pallas kernels  28.4 us (97%)
  local copies, waits for them, and re-layouts  0.8 us (3%)
    pallas_call x1, Pallas kernels, shards(): pl.pallas_call(functools.partial(kernel, (R, A, C)), out_shape=pltpu.VMEM...  28.4 us
    unnamed x1, local copies, waits for them, and re-layouts  0.8 us

profile of v2, /device:TPU:0, one launch (start us, length us, event | category | flops | bytes accessed | tf_op | source)
XLA Modules:
  0.0 29.2 jit_solution(10489650681410026759)
XLA Ops:
  0.0 28.4 %shard_map.37 = bf16[256,1024]{1,0:T(8,128)(2,1)S(1)} custom-call(bf16[256,256]{1,0:T(8,128)(2,1)} %density_ref.1, bf16[256,2048]{1,0:T(8,128)(2,1)} %panel_ref.1, s32[2,2]{1,0:T(2,128)} %pattern_hbm.1), custom_call_target="tpu_custom_call" | custom-call | tf_op jit(solution)/shard_map/pallas_call | solution.py:201
  28.4 0.8 %copy.5 = bf16[256,1024]{1,0:T(8,128)(2,1)} copy(bf16[256,1024]{1,0:T(8,128)(2,1)S(1)} %shard_map.37) | data formatting | bytes 1048576

commit v3 on v2

--- a/solution.py
+++ b/solution.py
@@ -15,7 +15,7 @@
 def kernel(
     sizes, density_ref, panel_ref, pattern_hbm, out_ref,
     pattern_ref, tile, fcol, frow, grow, p, acc,
-    load_sem, fc_s, fc_r, fr_s, fr_r, fs_s, fs_r, gr_s, gr_r, gs_s, gs_r,
+    load_sem, cx_s, cx_r, cy_s, cy_r, ex_s, ex_r, ey_s, ey_r, fr_s, fr_r, fs_s, fs_r, gr_s, gr_r, gs_s, gs_r,
     px_s, px_r, py_s, py_r, fx_s, fx_r, fy_s, fy_r,
 ):
     R, A, C = sizes
@@ -37,9 +37,17 @@
             device_id=dev, device_id_type=MESH,
         )
 
+    def x_peer(d):
+        return y * A + lax.rem(x + d, A)
+
+    def y_peer(d):
+        return lax.rem(y + d, B) * A + x
+
     barrier = pltpu.get_barrier_semaphore()
-    for d in range(1, R):
-        pl.semaphore_signal(barrier, inc=1, device_id={"row": lax.rem(r + d, R)}, device_id_type=MESH)
+    for d in range(1, A):
+        pl.semaphore_signal(barrier, inc=1, device_id={"row": x_peer(d)}, device_id_type=MESH)
+    for d in range(1, B):
+        pl.semaphore_signal(barrier, inc=1, device_id={"row": y_peer(d)}, device_id_type=MESH)
     for d in range(1, C):
         pl.semaphore_signal(barrier, inc=1, device_id={"col": lax.rem(c + d, C)}, device_id_type=MESH)
     pl.semaphore_signal(barrier, inc=1, device_id={"layer": sib}, device_id_type=MESH)
@@ -51,56 +59,88 @@
     own_cols = pl.ds(pl.multiple_of(l * W, W), W)
     load_panel = pltpu.make_async_copy(panel_ref.at[:, own_cols], p.at[r], load_sem.at[1])
     load_panel.start()
+    first, second = range(PIECES // 2), range(PIECES // 2, PIECES)
+
+    def cols_of(col, layer):
+        return pl.ds(pl.multiple_of(col * ti + layer * half, half), half)
+
+    def rows_of(row):
+        return pl.ds(pl.multiple_of(row * tr, tr), tr)
+
+    def half_rows(row, which):
+        return fcol.at[pl.ds(pl.multiple_of(row * tr + which * (tr // 2), tr // 2), tr // 2), :]
+
+    def piece(row, q):
+        return p.at[row, :, q * wq:(q + 1) * wq]
+
+    def x_source(d):
+        return y * A + lax.rem(x - d + A, A)
+
+    def y_source(d):
+        return lax.rem(y - d + B, B) * A + x
+
+    def both_source(dy, dx):
+        return lax.rem(y - dy + B, B) * A + lax.rem(x - dx + A, A)
+
+    sends = []
+
+    def send(ref, ssem, rsem, dev, src=None):
+        copy = pltpu.make_async_remote_copy(
+            src_ref=ref if src is None else src, dst_ref=ref, send_sem=ssem, recv_sem=rsem,
+            device_id=dev, device_id_type=MESH,
+        )
+        copy.start()
+        sends.append(copy)
+
+    def arrived(ref, ssem, rsem, dev):
+        rem_copy(ref, ssem, rsem, dev).wait_recv()
+
+    x_order = list(second) + list(first)
+    y_order = list(first) + list(second)
+
+    def send_own(n, from_hbm=False):
+        def src(q):
+            at = pl.ds(pl.multiple_of(l * W + q * wq, wq), wq)
+            return panel_ref.at[:, at] if from_hbm else None
+        qx, qy = x_order[n], y_order[n]
+        for d in range(1, A):
+            send(piece(r, qx), px_s.at[d, qx], px_r.at[d, qx], {"row": x_peer(d)}, src(qx))
+        for d in range(1, B):
+            send(piece(r, qy), py_s.at[d, qy], py_r.at[d, qy], {"row": y_peer(d)}, src(qy))
+
+    pl.semaphore_wait(barrier, A - 1 + B - 1 + C - 1 + 1)
+    send_own(0, from_hbm=True)
+
     load_pattern.wait()
     load_tile.wait()
-
     for a in range(tr // BS):
         for b in range(ti // BS):
             keep = pattern_ref[a, b].astype(jnp.float32)
             block = tile[a * BS:(a + 1) * BS, b * BS:(b + 1) * BS].astype(jnp.float32) * keep
             at = pl.ds(pl.multiple_of(c * ti + b * BS, BS), BS)
             frow[a * BS:(a + 1) * BS, at] = block.astype(jnp.bfloat16)
-    def cols_of(col, layer):
-        return pl.ds(pl.multiple_of(col * ti + layer * half, half), half)
-    def rows_of(row):
-        return pl.ds(pl.multiple_of(row * tr, tr), tr)
+    for d in range(1, C):
+        send(frow.at[:, cols_of(c, l)], fr_s.at[d], fr_r.at[d], {"col": lax.rem(c + d, C)})
     fcol[rows_of(r), :] = frow[:, cols_of(c, l)]
-
-    pl.semaphore_wait(barrier, R - 1 + C - 1 + 1)
-
-    sends = []
-
-    def send(ref, ssem, rsem, dev):
-        copy = rem_copy(ref, ssem, rsem, dev)
-        copy.start()
-        sends.append(copy)
-
-    def arrived(ref, ssem, rsem, dev):
-        rem_copy(ref, ssem, rsem, dev).wait_recv()
-
-    for d in range(1, R):
-        send(fcol.at[rows_of(r), :], fc_s.at[d], fc_r.at[d], {"row": lax.rem(r + d, R)})
-    for d in range(1, C):
-        send(frow.at[:, cols_of(c, l)], fr_s.at[d], fr_r.at[d], {"col": lax.rem(c + d, C)})
+    for d in range(1, A):
+        send(fcol.at[rows_of(r), :], cx_s.at[d], cx_r.at[d], {"row": x_peer(d)})
+    for d in range(1, B):
+        send(fcol.at[rows_of(r), :], cy_s.at[d], cy_r.at[d], {"row": y_peer(d)})
     load_panel.wait()
-    first, second = range(PIECES // 2), range(PIECES // 2, PIECES)
-
-    def piece(row, q):
-        return p.at[row, :, q * wq:(q + 1) * wq]
-
-    def x_peer(d):
-        return y * A + lax.rem(x + d, A)
-
-    def y_peer(d):
-        return lax.rem(y + d, B) * A + x
-
-    x_order = list(second) + list(first)
-    y_order = list(first) + list(second)
-    for qx, qy in zip(x_order, y_order):
-        for d in range(1, A):
-            send(piece(r, qx), px_s.at[d, qx], px_r.at[d, qx], {"row": x_peer(d)})
-        for d in range(1, B):
-            send(piece(r, qy), py_s.at[d, qy], py_r.at[d, qy], {"row": y_peer(d)})
+    send_own(1)
+
+    for dy in range(1, B):
+        row = y_source(dy)
+        arrived(fcol.at[rows_of(row), :], cy_s.at[dy], cy_r.at[dy], {"row": row})
+        for dx in range(1, A):
+            send(half_rows(row, 0), ex_s.at[dy, dx], ex_r.at[dy, dx], {"row": x_peer(dx)})
+    for dx in range(1, A):
+        row = x_source(dx)
+        arrived(fcol.at[rows_of(row), :], cx_s.at[dx], cx_r.at[dx], {"row": row})
+        for dy in range(1, B):
+            send(half_rows(row, 1), ey_s.at[dy, dx], ey_r.at[dy, dx], {"row": y_peer(dy)})
+    for n in range(2, PIECES):
+        send_own(n)
 
     for d in range(1, C):
         from_c = lax.rem(c - d + C, C)
@@ -110,9 +150,11 @@
     for d in range(1, C):
         from_c = lax.rem(c - d + C, C)
         arrived(frow.at[:, cols_of(from_c, sib)], fs_s.at[d], fs_r.at[d], {"layer": sib})
-    for d in range(1, R):
-        from_r = lax.rem(r - d + R, R)
-        arrived(fcol.at[rows_of(from_r), :], fc_s.at[d], fc_r.at[d], {"row": from_r})
+    for dy in range(1, B):
+        for dx in range(1, A):
+            row = both_source(dy, dx)
+            arrived(half_rows(row, 0), ex_s.at[dy, dx], ex_r.at[dy, dx], {"row": row})
+            arrived(half_rows(row, 1), ey_s.at[dy, dx], ey_r.at[dy, dx], {"row": row})
 
     grow[:, cols_of(c, l)] = jnp.dot(
         frow[...], fcol[...], preferred_element_type=jnp.float32
@@ -134,18 +176,20 @@
     for q in range(PIECES):
         acc[:, part(q)] = 3.0 * by(frow, r, q)
 
+    early = len(sends)
     for qf, qs in zip(first, second):
         for dy in range(1, B):
-            row = lax.rem(y - dy + B, B) * A + x
+            row = y_source(dy)
             arrived(piece(row, qf), py_s.at[dy, qf], py_r.at[dy, qf], {"row": row})
             for dx in range(1, A):
                 send(piece(row, qf), fx_s.at[dy, dx, qf], fx_r.at[dy, dx, qf], {"row": x_peer(dx)})
         for dx in range(1, A):
-            row = y * A + lax.rem(x - dx + A, A)
+            row = x_source(dx)
             arrived(piece(row, qs), px_s.at[dx, qs], px_r.at[dx, qs], {"row": row})
             for dy in range(1, B):
                 send(piece(row, qs), fy_s.at[dy, dx, qs], fy_r.at[dy, dx, qs], {"row": y_peer(dy)})
 
+    late = len(sends)
     for d in range(1, C):
         from_c = lax.rem(c - d + C, C)
         ref = grow.at[:, cols_of(from_c, l)]
@@ -158,31 +202,33 @@
     for q in range(PIECES):
         acc[:, part(q)] -= 2.0 * by(grow, r, q)
     for dx in range(1, A):
-        row = y * A + lax.rem(x - dx + A, A)
+        row = x_source(dx)
         for q in x_order:
             if q in first:
                 arrived(piece(row, q), px_s.at[dx, q], px_r.at[dx, q], {"row": row})
             acc[:, part(q)] += term(row, q)
     for dy in range(1, B):
-        row = lax.rem(y - dy + B, B) * A + x
+        row = y_source(dy)
         for q in y_order:
             if q in second:
                 arrived(piece(row, q), py_s.at[dy, q], py_r.at[dy, q], {"row": row})
             acc[:, part(q)] += term(row, q)
+    for copy in sends[:early] + sends[late:]:
+        copy.wait_send()
     for qf, qs in zip(first, second):
         for q, s_sem, r_sem in ((qf, fx_s, fx_r), (qs, fy_s, fy_r)):
             for dy in range(1, B):
                 for dx in range(1, A):
-                    row = lax.rem(y - dy + B, B) * A + lax.rem(x - dx + A, A)
+                    row = both_source(dy, dx)
                     arrived(piece(row, q), s_sem.at[dy, dx, q], r_sem.at[dy, dx, q], {"row": row})
             total = acc[:, part(q)]
             for dy in range(1, B):
                 for dx in range(1, A):
-                    row = lax.rem(y - dy + B, B) * A + lax.rem(x - dx + A, A)
+                    row = both_source(dy, dx)
                     total = total + term(row, q)
             out_ref[:, part(q)] = total.astype(jnp.bfloat16)
 
-    for copy in sends:
+    for copy in sends[early:late]:
         copy.wait_send()
 
 
@@ -212,7 +258,8 @@
             pltpu.VMEM((R, tr, W), bf16),
             pltpu.VMEM((tr, W), jnp.float32),
             dma((3,)),
-            dma((R,)), dma((R,)),
+            dma((A,)), dma((A,)), dma((B,)), dma((B,)),
+            dma((B, A)), dma((B, A)), dma((B, A)), dma((B, A)),
             dma((C,)), dma((C,)), dma((C,)), dma((C,)),
             dma((C,)), dma((C,)), dma((C,)), dma((C,)),
             dma((A, PIECES)), dma((A, PIECES)),

time: 29.3 us -> 28.9 us (0.986)
  Pallas kernels: 28.4 us -> 28 us
    pallas_call x1, Pallas kernels: 28.4 us -> 28 us  [shards(): pl.pallas_call(functools.partial(kernel, (R, A, C)), out_shape=pltpu.VMEM...]
where the time goes in v3:
time: 28.9 us; the launch traced here: 28.8 us
  Pallas kernels  28 us (97%)
  local copies, waits for them, and re-layouts  0.8 us (3%)
    pallas_call x1, Pallas kernels, shards(): pl.pallas_call(functools.partial(kernel, (R, A, C)), out_shape=pltpu.VMEM...  28 us
    unnamed x1, local copies, waits for them, and re-layouts  0.8 us

profile of v3, /device:TPU:0, one launch (start us, length us, event | category | flops | bytes accessed | tf_op | source)
XLA Modules:
  0.0 28.8 jit_solution(19195521062159466)
XLA Ops:
  0.0 28.0 %shard_map.37 = bf16[256,1024]{1,0:T(8,128)(2,1)S(1)} custom-call(bf16[256,256]{1,0:T(8,128)(2,1)} %density_ref.1, bf16[256,2048]{1,0:T(8,128)(2,1)} %panel_ref.1, s32[2,2]{1,0:T(2,128)} %pattern_hbm.1), custom_call_target="tpu_custom_call" | custom-call | tf_op jit(solution)/shard_map/pallas_call | solution.py:247
  28.0 0.8 %copy.5 = bf16[256,1024]{1,0:T(8,128)(2,1)} copy(bf16[256,1024]{1,0:T(8,128)(2,1)S(1)} %shard_map.37) | data formatting | bytes 1048576

commit v4 on v3

--- a/solution.py
+++ b/solution.py
@@ -22,7 +22,7 @@
     B = R // A
     tr, ti = density_ref.shape
     half = ti // 2
-    W = p.shape[2]
+    W = p.shape[1]
     wq = W // PIECES
     r = lax.axis_index("row")
     c = lax.axis_index("col")
@@ -57,30 +57,30 @@
     load_tile = pltpu.make_async_copy(density_ref, tile, load_sem.at[0])
     load_tile.start()
     own_cols = pl.ds(pl.multiple_of(l * W, W), W)
-    load_panel = pltpu.make_async_copy(panel_ref.at[:, own_cols], p.at[r], load_sem.at[1])
+    load_panel = pltpu.make_async_copy(panel_ref.at[:, own_cols], p.at[0:tr, :], load_sem.at[1])
     load_panel.start()
     first, second = range(PIECES // 2), range(PIECES // 2, PIECES)
 
-    def cols_of(col, layer):
-        return pl.ds(pl.multiple_of(col * ti + layer * half, half), half)
-
-    def rows_of(row):
-        return pl.ds(pl.multiple_of(row * tr, tr), tr)
-
-    def half_rows(row, which):
-        return fcol.at[pl.ds(pl.multiple_of(row * tr + which * (tr // 2), tr // 2), tr // 2), :]
-
-    def piece(row, q):
-        return p.at[row, :, q * wq:(q + 1) * wq]
+    def cols_of(col, layer, width=half, extra=0):
+        at = col * ti + layer * half + extra
+        row = at // tr
+        dy, dx = lax.rem(y - row // A + B, B), lax.rem(x - lax.rem(row, A) + A, A)
+        return pl.ds(pl.multiple_of((dy * A + dx) * tr + lax.rem(at, tr), width), width)
+
+    def rows_of(slot):
+        return slice(slot * tr, (slot + 1) * tr)
+
+    def half_rows(slot, which):
+        return fcol.at[slot * tr + which * (tr // 2):slot * tr + (which + 1) * (tr // 2), :]
+
+    def piece(slot, q):
+        return p.at[rows_of(slot), q * wq:(q + 1) * wq]
 
     def x_source(d):
         return y * A + lax.rem(x - d + A, A)
 
     def y_source(d):
         return lax.rem(y - d + B, B) * A + x
-
-    def both_source(dy, dx):
-        return lax.rem(y - dy + B, B) * A + lax.rem(x - dx + A, A)
 
     sends = []
 
@@ -101,12 +101,12 @@
     def send_own(n, from_hbm=False):
         def src(q):
             at = pl.ds(pl.multiple_of(l * W + q * wq, wq), wq)
-            return panel_ref.at[:, at] if from_hbm else None
+            return panel_ref.at[:, at] if from_hbm else piece(0, q)
         qx, qy = x_order[n], y_order[n]
         for d in range(1, A):
-            send(piece(r, qx), px_s.at[d, qx], px_r.at[d, qx], {"row": x_peer(d)}, src(qx))
+            send(piece(d, qx), px_s.at[d, qx], px_r.at[d, qx], {"row": x_peer(d)}, src(qx))
         for d in range(1, B):
-            send(piece(r, qy), py_s.at[d, qy], py_r.at[d, qy], {"row": y_peer(d)}, src(qy))
+            send(piece(d * A, qy), py_s.at[d, qy], py_r.at[d, qy], {"row": y_peer(d)}, src(qy))
 
     pl.semaphore_wait(barrier, A - 1 + B - 1 + C - 1 + 1)
     send_own(0, from_hbm=True)
@@ -117,28 +117,28 @@
         for b in range(ti // BS):
             keep = pattern_ref[a, b].astype(jnp.float32)
             block = tile[a * BS:(a + 1) * BS, b * BS:(b + 1) * BS].astype(jnp.float32) * keep
-            at = pl.ds(pl.multiple_of(c * ti + b * BS, BS), BS)
-            frow[a * BS:(a + 1) * BS, at] = block.astype(jnp.bfloat16)
+            frow[a * BS:(a + 1) * BS, cols_of(c, 0, BS, b * BS)] = block.astype(jnp.bfloat16)
     for d in range(1, C):
         send(frow.at[:, cols_of(c, l)], fr_s.at[d], fr_r.at[d], {"col": lax.rem(c + d, C)})
-    fcol[rows_of(r), :] = frow[:, cols_of(c, l)]
+    fcol[rows_of(0), :] = frow[:, cols_of(c, l)]
+    own_rows = fcol.at[rows_of(0), :]
     for d in range(1, A):
-        send(fcol.at[rows_of(r), :], cx_s.at[d], cx_r.at[d], {"row": x_peer(d)})
+        send(fcol.at[rows_of(d), :], cx_s.at[d], cx_r.at[d], {"row": x_peer(d)}, own_rows)
     for d in range(1, B):
-        send(fcol.at[rows_of(r), :], cy_s.at[d], cy_r.at[d], {"row": y_peer(d)})
+        send(fcol.at[rows_of(d * A), :], cy_s.at[d], cy_r.at[d], {"row": y_peer(d)}, own_rows)
     load_panel.wait()
     send_own(1)
 
     for dy in range(1, B):
-        row = y_source(dy)
-        arrived(fcol.at[rows_of(row), :], cy_s.at[dy], cy_r.at[dy], {"row": row})
-        for dx in range(1, A):
-            send(half_rows(row, 0), ex_s.at[dy, dx], ex_r.at[dy, dx], {"row": x_peer(dx)})
+        arrived(fcol.at[rows_of(dy * A), :], cy_s.at[dy], cy_r.at[dy], {"row": y_source(dy)})
+        for dx in range(1, A):
+            send(half_rows(dy * A + dx, 0), ex_s.at[dy, dx], ex_r.at[dy, dx], {"row": x_peer(dx)},
+                 half_rows(dy * A, 0))
     for dx in range(1, A):
-        row = x_source(dx)
-        arrived(fcol.at[rows_of(row), :], cx_s.at[dx], cx_r.at[dx], {"row": row})
-        for dy in range(1, B):
-            send(half_rows(row, 1), ey_s.at[dy, dx], ey_r.at[dy, dx], {"row": y_peer(dy)})
+        arrived(fcol.at[rows_of(dx), :], cx_s.at[dx], cx_r.at[dx], {"row": x_source(dx)})
+        for dy in range(1, B):
+            send(half_rows(dy * A + dx, 1), ey_s.at[dy, dx], ey_r.at[dy, dx], {"row": y_peer(dy)},
+                 half_rows(dx, 1))
     for n in range(2, PIECES):
         send_own(n)
 
@@ -152,9 +152,9 @@
         arrived(frow.at[:, cols_of(from_c, sib)], fs_s.at[d], fs_r.at[d], {"layer": sib})
     for dy in range(1, B):
         for dx in range(1, A):
-            row = both_source(dy, dx)
-            arrived(half_rows(row, 0), ex_s.at[dy, dx], ex_r.at[dy, dx], {"row": row})
-            arrived(half_rows(row, 1), ey_s.at[dy, dx], ey_r.at[dy, dx], {"row": row})
+            slot = dy * A + dx
+            arrived(half_rows(slot, 0), ex_s.at[dy, dx], ex_r.at[dy, dx], {"row": x_source(dx)})
+            arrived(half_rows(slot, 1), ey_s.at[dy, dx], ey_r.at[dy, dx], {"row": y_source(dy)})
 
     grow[:, cols_of(c, l)] = jnp.dot(
         frow[...], fcol[...], preferred_element_type=jnp.float32
@@ -166,66 +166,62 @@
     def part(q):
         return slice(q * wq, (q + 1) * wq)
 
-    def by(left, row, q):
-        at = pl.ds(pl.multiple_of(row * tr, tr), tr)
-        return jnp.dot(left[:, at], p[row, :, part(q)], preferred_element_type=jnp.float32)
-
-    def term(row, q):
-        return 3.0 * by(frow, row, q) - 2.0 * by(grow, row, q)
-
-    for q in range(PIECES):
-        acc[:, part(q)] = 3.0 * by(frow, r, q)
+    def by(left, group, q):
+        at = slice(group[0] * tr, group[1] * tr)
+        return jnp.dot(left[:, at], p[at, part(q)], preferred_element_type=jnp.float32)
+
+    near = [(0, A)]
+    for dy in range(1, B):
+        if dy * A == near[-1][1]:
+            near[-1] = (near[-1][0], dy * A + 1)
+        else:
+            near.append((dy * A, dy * A + 1))
+    far = [(dy * A + 1, dy * A + A) for dy in range(1, B)]
 
     early = len(sends)
     for qf, qs in zip(first, second):
         for dy in range(1, B):
-            row = y_source(dy)
-            arrived(piece(row, qf), py_s.at[dy, qf], py_r.at[dy, qf], {"row": row})
+            arrived(piece(dy * A, qf), py_s.at[dy, qf], py_r.at[dy, qf], {"row": y_source(dy)})
             for dx in range(1, A):
-                send(piece(row, qf), fx_s.at[dy, dx, qf], fx_r.at[dy, dx, qf], {"row": x_peer(dx)})
-        for dx in range(1, A):
-            row = x_source(dx)
-            arrived(piece(row, qs), px_s.at[dx, qs], px_r.at[dx, qs], {"row": row})
+                send(piece(dy * A + dx, qf), fx_s.at[dy, dx, qf], fx_r.at[dy, dx, qf],
+                     {"row": x_peer(dx)}, piece(dy * A, qf))
+        for dx in range(1, A):
+            arrived(piece(dx, qs), px_s.at[dx, qs], px_r.at[dx, qs], {"row": x_source(dx)})
             for dy in range(1, B):
-                send(piece(row, qs), fy_s.at[dy, dx, qs], fy_r.at[dy, dx, qs], {"row": y_peer(dy)})
-
+                send(piece(dy * A + dx, qs), fy_s.at[dy, dx, qs], fy_r.at[dy, dx, qs],
+                     {"row": y_peer(dy)}, piece(dx, qs))
     late = len(sends)
+
     for d in range(1, C):
         from_c = lax.rem(c - d + C, C)
         ref = grow.at[:, cols_of(from_c, l)]
         arrived(ref, gr_s.at[d], gr_r.at[d], {"col": from_c})
         send(ref, gs_s.at[d], gs_r.at[d], {"layer": sib})
+    for qf, qs in zip(first, second):
+        for dy in range(1, B):
+            arrived(piece(dy * A, qs), py_s.at[dy, qs], py_r.at[dy, qs], {"row": y_source(dy)})
+        for dx in range(1, A):
+            arrived(piece(dx, qf), px_s.at[dx, qf], px_r.at[dx, qf], {"row": x_source(dx)})
+        for q in (qf, qs):
+            acc[:, part(q)] = 3.0 * sum(by(frow, group, q) for group in near)
     for d in range(C):
         from_c = lax.rem(c - d + C, C)
         arrived(grow.at[:, cols_of(from_c, sib)], gs_s.at[d], gs_r.at[d], {"layer": sib})
-
     for q in range(PIECES):
-        acc[:, part(q)] -= 2.0 * by(grow, r, q)
-    for dx in range(1, A):
-        row = x_source(dx)
-        for q in x_order:
-            if q in first:
-                arrived(piece(row, q), px_s.at[dx, q], px_r.at[dx, q], {"row": row})
-            acc[:, part(q)] += term(row, q)
-    for dy in range(1, B):
-        row = y_source(dy)
-        for q in y_order:
-            if q in second:
-                arrived(piece(row, q), py_s.at[dy, q], py_r.at[dy, q], {"row": row})
-            acc[:, part(q)] += term(row, q)
+        acc[:, part(q)] -= 2.0 * sum(by(grow, group, q) for group in near)
+
     for copy in sends[:early] + sends[late:]:
         copy.wait_send()
     for qf, qs in zip(first, second):
-        for q, s_sem, r_sem in ((qf, fx_s, fx_r), (qs, fy_s, fy_r)):
-            for dy in range(1, B):
-                for dx in range(1, A):
-                    row = both_source(dy, dx)
-                    arrived(piece(row, q), s_sem.at[dy, dx, q], r_sem.at[dy, dx, q], {"row": row})
+        for dy in range(1, B):
+            for dx in range(1, A):
+                slot = dy * A + dx
+                arrived(piece(slot, qf), fx_s.at[dy, dx, qf], fx_r.at[dy, dx, qf], {"row": x_source(dx)})
+                arrived(piece(slot, qs), fy_s.at[dy, dx, qs], fy_r.at[dy, dx, qs], {"row": y_source(dy)})
+        for q in (qf, qs):
             total = acc[:, part(q)]
-            for dy in range(1, B):
-                for dx in range(1, A):
-                    row = both_source(dy, dx)
-                    total = total + term(row, q)
+            for group in far:
+                total = total + (3.0 * by(frow, group, q) - 2.0 * by(grow, group, q))
             out_ref[:, part(q)] = total.astype(jnp.bfloat16)
 
     for copy in sends[early:late]:
@@ -255,7 +251,7 @@
             pltpu.VMEM((K, half), bf16),
             pltpu.VMEM((tr, K), bf16),
             pltpu.VMEM((tr, K), bf16),
-            pltpu.VMEM((R, tr, W), bf16),
+            pltpu.VMEM((K, W), bf16),
             pltpu.VMEM((tr, W), jnp.float32),
             dma((3,)),
             dma((A,)), dma((A,)), dma((B,)), dma((B,)),

time: 28.9 us -> 28.8 us (level)
  no operation moved by 1% of the time
where the time goes in v4:
time: 28.8 us; the launch traced here: 28.6 us
  Pallas kernels  27.8 us (97%)
  local copies, waits for them, and re-layouts  0.8 us (3%)
    pallas_call x1, Pallas kernels, shards(): pl.pallas_call(functools.partial(kernel, (R, A, C)), out_shape=pltpu.VMEM...  27.8 us
    unnamed x1, local copies, waits for them, and re-layouts  0.8 us

profile of v4, /device:TPU:0, one launch (start us, length us, event | category | flops | bytes accessed | tf_op | source)
XLA Modules:
  0.0 28.6 jit_solution(9983788199275281394)
XLA Ops:
  0.0 27.8 %shard_map.37 = bf16[256,1024]{1,0:T(8,128)(2,1)S(1)} custom-call(bf16[256,256]{1,0:T(8,128)(2,1)} %density_ref.1, bf16[256,2048]{1,0:T(8,128)(2,1)} %panel_ref.1, s32[2,2]{1,0:T(2,128)} %pattern_hbm.1), custom_call_target="tpu_custom_call" | custom-call | tf_op jit(solution)/shard_map/pallas_call | solution.py:243
  27.8 0.8 %copy.5 = bf16[256,1024]{1,0:T(8,128)(2,1)} copy(bf16[256,1024]{1,0:T(8,128)(2,1)S(1)} %shard_map.37) | data formatting | bytes 1048576

commit v5 on v4

--- a/solution.py
+++ b/solution.py
@@ -98,18 +98,12 @@
     x_order = list(second) + list(first)
     y_order = list(first) + list(second)
 
-    def send_own(n, from_hbm=False):
-        def src(q):
-            at = pl.ds(pl.multiple_of(l * W + q * wq, wq), wq)
-            return panel_ref.at[:, at] if from_hbm else piece(0, q)
+    def send_own(n):
         qx, qy = x_order[n], y_order[n]
         for d in range(1, A):
-            send(piece(d, qx), px_s.at[d, qx], px_r.at[d, qx], {"row": x_peer(d)}, src(qx))
+            send(piece(d, qx), px_s.at[d, qx], px_r.at[d, qx], {"row": x_peer(d)}, piece(0, qx))
         for d in range(1, B):
-            send(piece(d * A, qy), py_s.at[d, qy], py_r.at[d, qy], {"row": y_peer(d)}, src(qy))
-
-    pl.semaphore_wait(barrier, A - 1 + B - 1 + C - 1 + 1)
-    send_own(0, from_hbm=True)
+            send(piece(d * A, qy), py_s.at[d, qy], py_r.at[d, qy], {"row": y_peer(d)}, piece(0, qy))
 
     load_pattern.wait()
     load_tile.wait()
@@ -118,15 +112,18 @@
             keep = pattern_ref[a, b].astype(jnp.float32)
             block = tile[a * BS:(a + 1) * BS, b * BS:(b + 1) * BS].astype(jnp.float32) * keep
             frow[a * BS:(a + 1) * BS, cols_of(c, 0, BS, b * BS)] = block.astype(jnp.bfloat16)
+    fcol[rows_of(0), :] = frow[:, cols_of(c, l)]
+
+    pl.semaphore_wait(barrier, A - 1 + B - 1 + C - 1 + 1)
     for d in range(1, C):
         send(frow.at[:, cols_of(c, l)], fr_s.at[d], fr_r.at[d], {"col": lax.rem(c + d, C)})
-    fcol[rows_of(0), :] = frow[:, cols_of(c, l)]
     own_rows = fcol.at[rows_of(0), :]
     for d in range(1, A):
         send(fcol.at[rows_of(d), :], cx_s.at[d], cx_r.at[d], {"row": x_peer(d)}, own_rows)
     for d in range(1, B):
         send(fcol.at[rows_of(d * A), :], cy_s.at[d], cy_r.at[d], {"row": y_peer(d)}, own_rows)
     load_panel.wait()
+    send_own(0)
     send_own(1)
 
     for dy in range(1, B):

time: 28.8 us -> 28.6 us (level)
  no operation moved by 1% of the time
where the time goes in v5:
time: 28.6 us; the launch traced here: 28.4 us
  Pallas kernels  27.6 us (97%)
  local copies, waits for them, and re-layouts  0.8 us (3%)
    pallas_call x1, Pallas kernels, shards(): pl.pallas_call(functools.partial(kernel, (R, A, C)), out_shape=pltpu.VMEM...  27.6 us
    unnamed x1, local copies, waits for them, and re-layouts  0.8 us

profile of v5, /device:TPU:0, one launch (start us, length us, event | category | flops | bytes accessed | tf_op | source)
XLA Modules:
  0.0 28.4 jit_solution(2690061520567362690)
XLA Ops:
  0.0 27.6 %shard_map.37 = bf16[256,1024]{1,0:T(8,128)(2,1)S(1)} custom-call(bf16[256,256]{1,0:T(8,128)(2,1)} %density_ref.1, bf16[256,2048]{1,0:T(8,128)(2,1)} %panel_ref.1, s32[2,2]{1,0:T(2,128)} %pattern_hbm.1), custom_call_target="tpu_custom_call" | custom-call | tf_op jit(solution)/shard_map/pallas_call | solution.py:240
  27.6 0.8 %copy.5 = bf16[256,1024]{1,0:T(8,128)(2,1)} copy(bf16[256,1024]{1,0:T(8,128)(2,1)S(1)} %shard_map.37) | data formatting | bytes 1048576

commit v6 on v5

--- a/solution.py
+++ b/solution.py
@@ -22,8 +22,8 @@
     B = R // A
     tr, ti = density_ref.shape
     half = ti // 2
-    W = p.shape[1]
-    wq = W // PIECES
+    wq = p.shape[2]
+    W = wq * PIECES
     r = lax.axis_index("row")
     c = lax.axis_index("col")
     l = lax.axis_index("layer")
@@ -52,13 +52,15 @@
         pl.semaphore_signal(barrier, inc=1, device_id={"col": lax.rem(c + d, C)}, device_id_type=MESH)
     pl.semaphore_signal(barrier, inc=1, device_id={"layer": sib}, device_id_type=MESH)
 
-    load_pattern = pltpu.make_async_copy(pattern_hbm, pattern_ref, load_sem.at[2])
+    load_pattern = pltpu.make_async_copy(pattern_hbm, pattern_ref, load_sem.at[1])
     load_pattern.start()
     load_tile = pltpu.make_async_copy(density_ref, tile, load_sem.at[0])
     load_tile.start()
-    own_cols = pl.ds(pl.multiple_of(l * W, W), W)
-    load_panel = pltpu.make_async_copy(panel_ref.at[:, own_cols], p.at[0:tr, :], load_sem.at[1])
-    load_panel.start()
+    load_panel = []
+    for q in range(PIECES):
+        at = pl.ds(pl.multiple_of(l * W + q * wq, wq), wq)
+        load_panel.append(pltpu.make_async_copy(panel_ref.at[:, at], p.at[q, 0:tr, :], load_sem.at[2 + q]))
+        load_panel[q].start()
     first, second = range(PIECES // 2), range(PIECES // 2, PIECES)
 
     def cols_of(col, layer, width=half, extra=0):
@@ -74,7 +76,7 @@
         return fcol.at[slot * tr + which * (tr // 2):slot * tr + (which + 1) * (tr // 2), :]
 
     def piece(slot, q):
-        return p.at[rows_of(slot), q * wq:(q + 1) * wq]
+        return p.at[q, rows_of(slot), :]
 
     def x_source(d):
         return y * A + lax.rem(x - d + A, A)
@@ -122,7 +124,8 @@
         send(fcol.at[rows_of(d), :], cx_s.at[d], cx_r.at[d], {"row": x_peer(d)}, own_rows)
     for d in range(1, B):
         send(fcol.at[rows_of(d * A), :], cy_s.at[d], cy_r.at[d], {"row": y_peer(d)}, own_rows)
-    load_panel.wait()
+    for copy in load_panel:
+        copy.wait()
     send_own(0)
     send_own(1)
 
@@ -165,7 +168,7 @@
 
     def by(left, group, q):
         at = slice(group[0] * tr, group[1] * tr)
-        return jnp.dot(left[:, at], p[at, part(q)], preferred_element_type=jnp.float32)
+        return jnp.dot(left[:, at], p[q, at, :], preferred_element_type=jnp.float32)
 
     near = [(0, A)]
     for dy in range(1, B):
@@ -248,9 +251,9 @@
             pltpu.VMEM((K, half), bf16),
             pltpu.VMEM((tr, K), bf16),
             pltpu.VMEM((tr, K), bf16),
-            pltpu.VMEM((K, W), bf16),
+            pltpu.VMEM((PIECES, K, W // PIECES), bf16),
             pltpu.VMEM((tr, W), jnp.float32),
-            dma((3,)),
+            dma((2 + PIECES,)),
             dma((A,)), dma((A,)), dma((B,)), dma((B,)),
             dma((B, A)), dma((B, A)), dma((B, A)), dma((B, A)),
             dma((C,)), dma((C,)), dma((C,)), dma((C,)),

time: 28.6 us -> 28.6 us (level)
  no operation moved by 1% of the time
where the time goes in v6:
time: 28.6 us; the launch traced here: 28.5 us
  Pallas kernels  27.7 us (97%)
  local copies, waits for them, and re-layouts  0.8 us (3%)
    pallas_call x1, Pallas kernels, shards(): pl.pallas_call(functools.partial(kernel, (R, A, C)), out_shape=pltpu.VMEM...  27.7 us
    unnamed x1, local copies, waits for them, and re-layouts  0.8 us

profile of v6, /device:TPU:0, one launch (start us, length us, event | category | flops | bytes accessed | tf_op | source)
XLA Modules:
  0.0 28.5 jit_solution(5610759015364683421)
XLA Ops:
  0.0 27.7 %shard_map.37 = bf16[256,1024]{1,0:T(8,128)(2,1)S(1)} custom-call(bf16[256,256]{1,0:T(8,128)(2,1)} %density_ref.1, bf16[256,2048]{1,0:T(8,128)(2,1)} %panel_ref.1, s32[2,2]{1,0:T(2,128)} %pattern_hbm.1), custom_call_target="tpu_custom_call" | custom-call | tf_op jit(solution)/shard_map/pallas_call | solution.py:243
  27.7 0.8 %copy.5 = bf16[256,1024]{1,0:T(8,128)(2,1)} copy(bf16[256,1024]{1,0:T(8,128)(2,1)S(1)} %shard_map.37) | data formatting | bytes 1048576

commit v7 on v6

--- a/solution.py
+++ b/solution.py
@@ -139,7 +139,7 @@
         for dy in range(1, B):
             send(half_rows(dy * A + dx, 1), ey_s.at[dy, dx], ey_r.at[dy, dx], {"row": y_peer(dy)},
                  half_rows(dx, 1))
-    for n in range(2, PIECES):
+    for n in range(2, PIECES - 1):
         send_own(n)
 
     for d in range(1, C):
@@ -147,6 +147,7 @@
         ref = frow.at[:, cols_of(from_c, l)]
         arrived(ref, fr_s.at[d], fr_r.at[d], {"col": from_c})
         send(ref, fs_s.at[d], fs_r.at[d], {"layer": sib})
+    send_own(PIECES - 1)
     for d in range(1, C):
         from_c = lax.rem(c - d + C, C)
         arrived(frow.at[:, cols_of(from_c, sib)], fs_s.at[d], fs_r.at[d], {"layer": sib})

time: 28.6 us -> 28.6 us (level)
  no operation moved by 1% of the time
where the time goes in v7:
time: 28.6 us; the launch traced here: 28.5 us
  Pallas kernels  27.7 us (97%)
  local copies, waits for them, and re-layouts  0.8 us (3%)
    pallas_call x1, Pallas kernels, shards(): pl.pallas_call(functools.partial(kernel, (R, A, C)), out_shape=pltpu.VMEM...  27.7 us
    unnamed x1, local copies, waits for them, and re-layouts  0.8 us

profile of v7, /device:TPU:0, one launch (start us, length us, event | category | flops | bytes accessed | tf_op | source)
XLA Modules:
  0.0 28.5 jit_solution(15542780099806843925)
XLA Ops:
  0.0 27.7 %shard_map.37 = bf16[256,1024]{1,0:T(8,128)(2,1)S(1)} custom-call(bf16[256,256]{1,0:T(8,128)(2,1)} %density_ref.1, bf16[256,2048]{1,0:T(8,128)(2,1)} %panel_ref.1, s32[2,2]{1,0:T(2,128)} %pattern_hbm.1), custom_call_target="tpu_custom_call" | custom-call | tf_op jit(solution)/shard_map/pallas_call | solution.py:244
  27.7 0.8 %copy.5 = bf16[256,1024]{1,0:T(8,128)(2,1)} copy(bf16[256,1024]{1,0:T(8,128)(2,1)S(1)} %shard_map.37) | data formatting | bytes 1048576

commit v8 on v7

--- a/solution.py
+++ b/solution.py
@@ -15,13 +15,16 @@
 def kernel(
     sizes, density_ref, panel_ref, pattern_hbm, out_ref,
     pattern_ref, tile, fcol, frow, grow, p, acc,
-    load_sem, cx_s, cx_r, cy_s, cy_r, ex_s, ex_r, ey_s, ey_r, fr_s, fr_r, fs_s, fs_r, gr_s, gr_r, gs_s, gs_r,
+    load_sem, cx_s, cx_r, cy_s, cy_r, ex_s, ex_r, ey_s, ey_r, cs_s, cs_r, fr_s, fr_r, fs_s, fs_r, gr_s, gr_r, gs_s, gs_r,
     px_s, px_r, py_s, py_r, fx_s, fx_r, fy_s, fy_r,
 ):
     R, A, C = sizes
     B = R // A
     tr, ti = density_ref.shape
     half = ti // 2
+    hr = tr // 2
+    block = min(ti, tr)
+    blocks = range(ti // block)
     wq = p.shape[2]
     W = wq * PIECES
     r = lax.axis_index("row")
@@ -63,8 +66,8 @@
         load_panel[q].start()
     first, second = range(PIECES // 2), range(PIECES // 2, PIECES)
 
-    def cols_of(col, layer, width=half, extra=0):
-        at = col * ti + layer * half + extra
+    def cols_of(col, extra=0, width=block):
+        at = col * ti + extra
         row = at // tr
         dy, dx = lax.rem(y - row // A + B, B), lax.rem(x - lax.rem(row, A) + A, A)
         return pl.ds(pl.multiple_of((dy * A + dx) * tr + lax.rem(at, tr), width), width)
@@ -72,8 +75,19 @@
     def rows_of(slot):
         return slice(slot * tr, (slot + 1) * tr)
 
+    own_half = pl.ds(pl.multiple_of(l * half, half), half)
+
+    def column(slot):
+        return fcol.at[rows_of(slot), own_half]
+
     def half_rows(slot, which):
-        return fcol.at[slot * tr + which * (tr // 2):slot * tr + (which + 1) * (tr // 2), :]
+        return fcol.at[slot * tr + which * hr:slot * tr + (which + 1) * hr, own_half]
+
+    def half_of(layer):
+        return pl.ds(pl.multiple_of(layer * hr, hr), hr)
+
+    def row_tile(buf, col, layer, j):
+        return buf.at[half_of(layer), cols_of(col, j * block)]
 
     def piece(slot, q):
         return p.at[q, rows_of(slot), :]
@@ -112,64 +126,73 @@
     for a in range(tr // BS):
         for b in range(ti // BS):
             keep = pattern_ref[a, b].astype(jnp.float32)
-            block = tile[a * BS:(a + 1) * BS, b * BS:(b + 1) * BS].astype(jnp.float32) * keep
-            frow[a * BS:(a + 1) * BS, cols_of(c, 0, BS, b * BS)] = block.astype(jnp.bfloat16)
-    fcol[rows_of(0), :] = frow[:, cols_of(c, l)]
+            masked = tile[a * BS:(a + 1) * BS, b * BS:(b + 1) * BS].astype(jnp.float32) * keep
+            frow[a * BS:(a + 1) * BS, cols_of(c, b * BS, BS)] = masked.astype(jnp.bfloat16)
+    for j in blocks:
+        fcol[rows_of(0), j * block:(j + 1) * block] = frow[:, cols_of(c, j * block)]
 
     pl.semaphore_wait(barrier, A - 1 + B - 1 + C - 1 + 1)
     for d in range(1, C):
-        send(frow.at[:, cols_of(c, l)], fr_s.at[d], fr_r.at[d], {"col": lax.rem(c + d, C)})
-    own_rows = fcol.at[rows_of(0), :]
+        for j in blocks:
+            send(row_tile(frow, c, l, j), fr_s.at[d, j], fr_r.at[d, j], {"col": lax.rem(c + d, C)})
+    own_rows = column(0)
     for d in range(1, A):
-        send(fcol.at[rows_of(d), :], cx_s.at[d], cx_r.at[d], {"row": x_peer(d)}, own_rows)
+        send(column(d), cx_s.at[d], cx_r.at[d], {"row": x_peer(d)}, own_rows)
     for d in range(1, B):
-        send(fcol.at[rows_of(d * A), :], cy_s.at[d], cy_r.at[d], {"row": y_peer(d)}, own_rows)
+        send(column(d * A), cy_s.at[d], cy_r.at[d], {"row": y_peer(d)}, own_rows)
     for copy in load_panel:
         copy.wait()
     send_own(0)
     send_own(1)
 
     for dy in range(1, B):
-        arrived(fcol.at[rows_of(dy * A), :], cy_s.at[dy], cy_r.at[dy], {"row": y_source(dy)})
+        arrived(column(dy * A), cy_s.at[dy], cy_r.at[dy], {"row": y_source(dy)})
+        send(column(dy * A), cs_s.at[dy * A], cs_r.at[dy * A], {"layer": sib})
         for dx in range(1, A):
             send(half_rows(dy * A + dx, 0), ex_s.at[dy, dx], ex_r.at[dy, dx], {"row": x_peer(dx)},
                  half_rows(dy * A, 0))
     for dx in range(1, A):
-        arrived(fcol.at[rows_of(dx), :], cx_s.at[dx], cx_r.at[dx], {"row": x_source(dx)})
+        arrived(column(dx), cx_s.at[dx], cx_r.at[dx], {"row": x_source(dx)})
+        send(column(dx), cs_s.at[dx], cs_r.at[dx], {"layer": sib})
         for dy in range(1, B):
             send(half_rows(dy * A + dx, 1), ey_s.at[dy, dx], ey_r.at[dy, dx], {"row": y_peer(dy)},
                  half_rows(dx, 1))
     for n in range(2, PIECES - 1):
         send_own(n)
 
-    for d in range(1, C):
-        from_c = lax.rem(c - d + C, C)
-        ref = frow.at[:, cols_of(from_c, l)]
-        arrived(ref, fr_s.at[d], fr_r.at[d], {"col": from_c})
-        send(ref, fs_s.at[d], fs_r.at[d], {"layer": sib})
-    send_own(PIECES - 1)
-    for d in range(1, C):
-        from_c = lax.rem(c - d + C, C)
-        arrived(frow.at[:, cols_of(from_c, sib)], fs_s.at[d], fs_r.at[d], {"layer": sib})
     for dy in range(1, B):
         for dx in range(1, A):
             slot = dy * A + dx
             arrived(half_rows(slot, 0), ex_s.at[dy, dx], ex_r.at[dy, dx], {"row": x_source(dx)})
             arrived(half_rows(slot, 1), ey_s.at[dy, dx], ey_r.at[dy, dx], {"row": y_source(dy)})
-
-    grow[:, cols_of(c, l)] = jnp.dot(
-        frow[...], fcol[...], preferred_element_type=jnp.float32
-    ).astype(jnp.bfloat16)
-    for d in range(1, C):
-        send(grow.at[:, cols_of(c, l)], gr_s.at[d], gr_r.at[d], {"col": lax.rem(c + d, C)})
-    send(grow.at[:, cols_of(c, l)], gs_s.at[0], gs_r.at[0], {"layer": sib})
+            send(column(slot), cs_s.at[slot], cs_r.at[slot], {"layer": sib})
+
+    for d in range(1, C):
+        from_c = lax.rem(c - d + C, C)
+        for j in blocks:
+            ref = row_tile(frow, from_c, l, j)
+            arrived(ref, fr_s.at[d, j], fr_r.at[d, j], {"col": from_c})
+            send(ref, fs_s.at[d, j], fs_r.at[d, j], {"layer": sib})
+    send_own(PIECES - 1)
+    other_half = pl.ds(pl.multiple_of(sib * half, half), half)
+    for slot in range(1, R):
+        arrived(fcol.at[rows_of(slot), other_half], cs_s.at[slot], cs_r.at[slot], {"layer": sib})
+
+    for j in blocks:
+        grow[half_of(l), cols_of(c, j * block)] = jnp.dot(
+            frow[half_of(l), :], fcol[:, j * block:(j + 1) * block], preferred_element_type=jnp.float32
+        ).astype(jnp.bfloat16)
+        ref = row_tile(grow, c, l, j)
+        for d in range(1, C):
+            send(ref, gr_s.at[d, j], gr_r.at[d, j], {"col": lax.rem(c + d, C)})
+        send(ref, gs_s.at[0, j], gs_r.at[0, j], {"layer": sib})
 
     def part(q):
         return slice(q * wq, (q + 1) * wq)
 
-    def by(left, group, q):
+    def by(left, group, q, rows=slice(None)):
         at = slice(group[0] * tr, group[1] * tr)
-        return jnp.dot(left[:, at], p[q, at, :], preferred_element_type=jnp.float32)
+        return jnp.dot(left[rows, at], p[q, at, :], preferred_element_type=jnp.float32)
 
     near = [(0, A)]
     for dy in range(1, B):
@@ -195,9 +218,14 @@
 
     for d in range(1, C):
         from_c = lax.rem(c - d + C, C)
-        ref = grow.at[:, cols_of(from_c, l)]
-        arrived(ref, gr_s.at[d], gr_r.at[d], {"col": from_c})
-        send(ref, gs_s.at[d], gs_r.at[d], {"layer": sib})
+        for j in blocks:
+            ref = row_tile(grow, from_c, l, j)
+            arrived(ref, gr_s.at[d, j], gr_r.at[d, j], {"col": from_c})
+            send(ref, gs_s.at[d, j], gs_r.at[d, j], {"layer": sib})
+    for d in range(1, C):
+        from_c = lax.rem(c - d + C, C)
+        for j in blocks:
+            arrived(row_tile(frow, from_c, sib, j), fs_s.at[d, j], fs_r.at[d, j], {"layer": sib})
     for qf, qs in zip(first, second):
         for dy in range(1, B):
             arrived(piece(dy * A, qs), py_s.at[dy, qs], py_r.at[dy, qs], {"row": y_source(dy)})
@@ -205,11 +233,14 @@
             arrived(piece(dx, qf), px_s.at[dx, qf], px_r.at[dx, qf], {"row": x_source(dx)})
         for q in (qf, qs):
             acc[:, part(q)] = 3.0 * sum(by(frow, group, q) for group in near)
+    for q in range(PIECES):
+        acc[half_of(l), part(q)] -= 2.0 * sum(by(grow, group, q, half_of(l)) for group in near)
     for d in range(C):
         from_c = lax.rem(c - d + C, C)
-        arrived(grow.at[:, cols_of(from_c, sib)], gs_s.at[d], gs_r.at[d], {"layer": sib})
+        for j in blocks:
+            arrived(row_tile(grow, from_c, sib, j), gs_s.at[d, j], gs_r.at[d, j], {"layer": sib})
     for q in range(PIECES):
-        acc[:, part(q)] -= 2.0 * sum(by(grow, group, q) for group in near)
+        acc[half_of(sib), part(q)] -= 2.0 * sum(by(grow, group, q, half_of(sib)) for group in near)
 
     for copy in sends[:early] + sends[late:]:
         copy.wait_send()
@@ -235,7 +266,7 @@
         A *= 2
     B = R // A
     tr, ti = density.shape
-    half = ti // L
+    nb = max(ti // tr, 1)
     W = panel.shape[1] // L
     K = tr * R
     dma = pltpu.SemaphoreType.DMA
@@ -249,7 +280,7 @@
         scratch_shapes=[
             pltpu.SMEM(pattern.shape, jnp.int32),
             pltpu.VMEM((tr, ti), bf16),
-            pltpu.VMEM((K, half), bf16),
+            pltpu.VMEM((K, ti), bf16),
             pltpu.VMEM((tr, K), bf16),
             pltpu.VMEM((tr, K), bf16),
             pltpu.VMEM((PIECES, K, W // PIECES), bf16),
@@ -257,8 +288,9 @@
             dma((2 + PIECES,)),
             dma((A,)), dma((A,)), dma((B,)), dma((B,)),
             dma((B, A)), dma((B, A)), dma((B, A)), dma((B, A)),
-            dma((C,)), dma((C,)), dma((C,)), dma((C,)),
-            dma((C,)), dma((C,)), dma((C,)), dma((C,)),
+            dma((R,)), dma((R,)),
+            dma((C, nb)), dma((C, nb)), dma((C, nb)), dma((C, nb)),
+            dma((C, nb)), dma((C, nb)), dma((C, nb)), dma((C, nb)),
             dma((A, PIECES)), dma((A, PIECES)),
             dma((B, PIECES)), dma((B, PIECES)),
             dma((B, A, PIECES)), dma((B, A, PIECES)),

time: 28.6 us -> 28.7 us (level)
  no operation moved by 1% of the time
where the time goes in v8:
time: 28.7 us; the launch traced here: 28.5 us
  Pallas kernels  27.7 us (97%)
  local copies, waits for them, and re-layouts  0.8 us (3%)
    pallas_call x1, Pallas kernels, shards(): pl.pallas_call(functools.partial(kernel, (R, A, C)), out_shape=pltpu.VMEM...  27.7 us
    unnamed x1, local copies, waits for them, and re-layouts  0.8 us

profile of v8, /device:TPU:0, one launch (start us, length us, event | category | flops | bytes accessed | tf_op | source)
XLA Modules:
  0.0 28.5 jit_solution(11264378995072075684)
XLA Ops:
  0.0 27.7 %shard_map.37 = bf16[256,1024]{1,0:T(8,128)(2,1)S(1)} custom-call(bf16[256,256]{1,0:T(8,128)(2,1)} %density_ref.1, bf16[256,2048]{1,0:T(8,128)(2,1)} %panel_ref.1, s32[2,2]{1,0:T(2,128)} %pattern_hbm.1), custom_call_target="tpu_custom_call" | custom-call | tf_op jit(solution)/shard_map/pallas_call | solution.py:275
  27.7 0.8 %copy.5 = bf16[256,1024]{1,0:T(8,128)(2,1)} copy(bf16[256,1024]{1,0:T(8,128)(2,1)S(1)} %shard_map.37) | data formatting | bytes 1048576

commit v9 on v6

--- a/solution.py
+++ b/solution.py
@@ -15,7 +15,7 @@
 def kernel(
     sizes, density_ref, panel_ref, pattern_hbm, out_ref,
     pattern_ref, tile, fcol, frow, grow, p, acc,
-    load_sem, cx_s, cx_r, cy_s, cy_r, ex_s, ex_r, ey_s, ey_r, fr_s, fr_r, fs_s, fs_r, gr_s, gr_r, gs_s, gs_r,
+    go, load_sem, cx_s, cx_r, cy_s, cy_r, ex_s, ex_r, ey_s, ey_r, fr_s, fr_r, fs_s, fs_r, gr_s, gr_r, gs_s, gs_r,
     px_s, px_r, py_s, py_r, fx_s, fx_r, fy_s, fy_r,
 ):
     R, A, C = sizes
@@ -44,13 +44,21 @@
         return lax.rem(y + d, B) * A + x
 
     barrier = pltpu.get_barrier_semaphore()
-    for d in range(1, A):
-        pl.semaphore_signal(barrier, inc=1, device_id={"row": x_peer(d)}, device_id_type=MESH)
-    for d in range(1, B):
-        pl.semaphore_signal(barrier, inc=1, device_id={"row": y_peer(d)}, device_id_type=MESH)
-    for d in range(1, C):
-        pl.semaphore_signal(barrier, inc=1, device_id={"col": lax.rem(c + d, C)}, device_id_type=MESH)
-    pl.semaphore_signal(barrier, inc=1, device_id={"layer": sib}, device_id_type=MESH)
+    def greet(sem, peers):
+        for peer in peers:
+            pl.semaphore_signal(sem, inc=1, device_id=peer, device_id_type=MESH)
+
+    row_peers = [{"row": x_peer(d)} for d in range(1, A)] + [{"row": y_peer(d)} for d in range(1, B)]
+    col_peers = [{"col": lax.rem(c + d, C)} for d in range(1, C)]
+    sibling = [{"layer": sib}]
+
+    @pl.when(l == 0)
+    def _():
+        greet(barrier, row_peers + sibling)
+
+    @pl.when(l == 1)
+    def _():
+        greet(barrier, col_peers + sibling)
 
     load_pattern = pltpu.make_async_copy(pattern_hbm, pattern_ref, load_sem.at[1])
     load_pattern.start()
@@ -86,13 +94,16 @@
 
     sends = []
 
-    def send(ref, ssem, rsem, dev, src=None):
+    def prepare(ref, ssem, rsem, dev, src=None):
         copy = pltpu.make_async_remote_copy(
             src_ref=ref if src is None else src, dst_ref=ref, send_sem=ssem, recv_sem=rsem,
             device_id=dev, device_id_type=MESH,
         )
-        copy.start()
         sends.append(copy)
+        return copy
+
+    def send(*args):
+        prepare(*args).start()
 
     def arrived(ref, ssem, rsem, dev):
         rem_copy(ref, ssem, rsem, dev).wait_recv()
@@ -100,12 +111,15 @@
     x_order = list(second) + list(first)
     y_order = list(first) + list(second)
 
-    def send_own(n):
+    def own_piece(n):
         qx, qy = x_order[n], y_order[n]
-        for d in range(1, A):
-            send(piece(d, qx), px_s.at[d, qx], px_r.at[d, qx], {"row": x_peer(d)}, piece(0, qx))
-        for d in range(1, B):
-            send(piece(d * A, qy), py_s.at[d, qy], py_r.at[d, qy], {"row": y_peer(d)}, piece(0, qy))
+        return [
+            prepare(piece(d, qx), px_s.at[d, qx], px_r.at[d, qx], {"row": x_peer(d)}, piece(0, qx))
+            for d in range(1, A)
+        ] + [
+            prepare(piece(d * A, qy), py_s.at[d, qy], py_r.at[d, qy], {"row": y_peer(d)}, piece(0, qy))
+            for d in range(1, B)
+        ]
 
     load_pattern.wait()
     load_tile.wait()
@@ -116,18 +130,46 @@
             frow[a * BS:(a + 1) * BS, cols_of(c, 0, BS, b * BS)] = block.astype(jnp.bfloat16)
     fcol[rows_of(0), :] = frow[:, cols_of(c, l)]
 
-    pl.semaphore_wait(barrier, A - 1 + B - 1 + C - 1 + 1)
-    for d in range(1, C):
-        send(frow.at[:, cols_of(c, l)], fr_s.at[d], fr_r.at[d], {"col": lax.rem(c + d, C)})
     own_rows = fcol.at[rows_of(0), :]
-    for d in range(1, A):
-        send(fcol.at[rows_of(d), :], cx_s.at[d], cx_r.at[d], {"row": x_peer(d)}, own_rows)
-    for d in range(1, B):
-        send(fcol.at[rows_of(d * A), :], cy_s.at[d], cy_r.at[d], {"row": y_peer(d)}, own_rows)
+    over_col = [
+        prepare(frow.at[:, cols_of(c, l)], fr_s.at[d], fr_r.at[d], {"col": lax.rem(c + d, C)})
+        for d in range(1, C)
+    ]
+    over_row = [
+        prepare(fcol.at[rows_of(d), :], cx_s.at[d], cx_r.at[d], {"row": x_peer(d)}, own_rows)
+        for d in range(1, A)
+    ] + [
+        prepare(fcol.at[rows_of(d * A), :], cy_s.at[d], cy_r.at[d], {"row": y_peer(d)}, own_rows)
+        for d in range(1, B)
+    ]
+    for n in range(PIECES):
+        over_row += own_piece(n)
     for copy in load_panel:
         copy.wait()
-    send_own(0)
-    send_own(1)
+
+    @pl.when(l == 0)
+    def _():
+        pl.semaphore_wait(barrier, len(row_peers) + 1)
+        greet(go.at[0], row_peers)
+        for copy in over_row:
+            copy.start()
+        pl.semaphore_wait(go.at[0], len(row_peers))
+        greet(go.at[2], sibling)
+        pl.semaphore_wait(go.at[2], 1)
+        for copy in over_col:
+            copy.start()
+
+    @pl.when(l == 1)
+    def _():
+        pl.semaphore_wait(barrier, len(col_peers) + 1)
+        greet(go.at[1], col_peers)
+        for copy in over_col:
+            copy.start()
+        pl.semaphore_wait(go.at[1], len(col_peers))
+        greet(go.at[2], sibling)
+        pl.semaphore_wait(go.at[2], 1)
+        for copy in over_row:
+            copy.start()
 
     for dy in range(1, B):
         arrived(fcol.at[rows_of(dy * A), :], cy_s.at[dy], cy_r.at[dy], {"row": y_source(dy)})
@@ -139,8 +181,6 @@
         for dy in range(1, B):
             send(half_rows(dy * A + dx, 1), ey_s.at[dy, dx], ey_r.at[dy, dx], {"row": y_peer(dy)},
                  half_rows(dx, 1))
-    for n in range(2, PIECES):
-        send_own(n)
 
     for d in range(1, C):
         from_c = lax.rem(c - d + C, C)
@@ -253,6 +293,7 @@
             pltpu.VMEM((tr, K), bf16),
             pltpu.VMEM((PIECES, K, W // PIECES), bf16),
             pltpu.VMEM((tr, W), jnp.float32),
+            pltpu.SemaphoreType.REGULAR((3,)),
             dma((2 + PIECES,)),
             dma((A,)), dma((A,)), dma((B,)), dma((B,)),
             dma((B, A)), dma((B, A)), dma((B, A)), dma((B, A)),

time: 28.6 us -> 31.5 us (1.10)
  Pallas kernels: 27.7 us -> 30.5 us
    pallas_call x1, Pallas kernels: 27.7 us -> 30.5 us  [shards(): pl.pallas_call(functools.partial(kernel, (R, A, C)), out_shape=pltpu.VMEM...]
where the time goes in v9:
time: 31.5 us; the launch traced here: 31.3 us
  Pallas kernels  30.5 us (97%)
  local copies, waits for them, and re-layouts  0.8 us (3%)
    pallas_call x1, Pallas kernels, shards(): pl.pallas_call(functools.partial(kernel, (R, A, C)), out_shape=pltpu.VMEM...  30.5 us
    unnamed x1, local copies, waits for them, and re-layouts  0.8 us

profile of v9, /device:TPU:0, one launch (start us, length us, event | category | flops | bytes accessed | tf_op | source)
XLA Modules:
  0.0 31.3 jit_solution(16146647867516516670)
XLA Ops:
  0.0 30.5 %shard_map.37 = bf16[256,1024]{1,0:T(8,128)(2,1)S(1)} custom-call(bf16[256,256]{1,0:T(8,128)(2,1)} %density_ref.1, bf16[256,2048]{1,0:T(8,128)(2,1)} %panel_ref.1, s32[2,2]{1,0:T(2,128)} %pattern_hbm.1), custom_call_target="tpu_custom_call" | custom-call | tf_op jit(solution)/shard_map/pallas_call | solution.py:283
  30.5 0.8 %copy.5 = bf16[256,1024]{1,0:T(8,128)(2,1)} copy(bf16[256,1024]{1,0:T(8,128)(2,1)S(1)} %shard_map.37) | data formatting | bytes 1048576

commit v10 on v9

--- a/solution.py
+++ b/solution.py
@@ -142,7 +142,7 @@
         prepare(fcol.at[rows_of(d * A), :], cy_s.at[d], cy_r.at[d], {"row": y_peer(d)}, own_rows)
         for d in range(1, B)
     ]
-    for n in range(PIECES):
+    for n in range(2):
         over_row += own_piece(n)
     for copy in load_panel:
         copy.wait()
@@ -181,6 +181,10 @@
         for dy in range(1, B):
             send(half_rows(dy * A + dx, 1), ey_s.at[dy, dx], ey_r.at[dy, dx], {"row": y_peer(dy)},
                  half_rows(dx, 1))
+
+    for n in range(2, PIECES):
+        for copy in own_piece(n):
+            copy.start()
 
     for d in range(1, C):
         from_c = lax.rem(c - d + C, C)

time: 31.5 us -> 27 us (0.86)
  the two profiles are of different devices: /device:TPU:0 before, /device:TPU:1 now
where the time goes in v10:
time: 27 us; the launch traced here: 26.9 us
  Pallas kernels  26.1 us (97%)
  local copies, waits for them, and re-layouts  0.8 us (3%)
    pallas_call x1, Pallas kernels, shards(): pl.pallas_call(functools.partial(kernel, (R, A, C)), out_shape=pltpu.VMEM...  26.1 us
    unnamed x1, local copies, waits for them, and re-layouts  0.8 us

profile of v10, /device:TPU:1, one launch (start us, length us, event | category | flops | bytes accessed | tf_op | source)
XLA Modules:
  0.0 26.9 jit_solution(16965425094548242803)
XLA Ops:
  0.0 26.1 %shard_map.37 = bf16[256,1024]{1,0:T(8,128)(2,1)S(1)} custom-call(bf16[256,256]{1,0:T(8,128)(2,1)} %density_ref.1, bf16[256,2048]{1,0:T(8,128)(2,1)} %panel_ref.1, s32[2,2]{1,0:T(2,128)} %pattern_hbm.1), custom_call_target="tpu_custom_call" | custom-call | tf_op jit(solution)/shard_map/pallas_call | solution.py:287
  26.1 0.8 %copy.5 = bf16[256,1024]{1,0:T(8,128)(2,1)} copy(bf16[256,1024]{1,0:T(8,128)(2,1)S(1)} %shard_map.37) | data formatting | bytes 1048576

commit v11 on v10

--- a/solution.py
+++ b/solution.py
@@ -161,15 +161,15 @@
 
     @pl.when(l == 1)
     def _():
+        pl.semaphore_wait(go.at[2], 1)
+        for copy in over_row:
+            copy.start()
         pl.semaphore_wait(barrier, len(col_peers) + 1)
         greet(go.at[1], col_peers)
         for copy in over_col:
             copy.start()
         pl.semaphore_wait(go.at[1], len(col_peers))
         greet(go.at[2], sibling)
-        pl.semaphore_wait(go.at[2], 1)
-        for copy in over_row:
-            copy.start()
 
     for dy in range(1, B):
         arrived(fcol.at[rows_of(dy * A), :], cy_s.at[dy], cy_r.at[dy], {"row": y_source(dy)})

time: 27 us -> 27 us (level)
  the two profiles are of different devices: /device:TPU:1 before, /device:TPU:0 now
where the time goes in v11:
time: 27 us; the launch traced here: 26.5 us
  Pallas kernels  25.7 us (95%)
  local copies, waits for them, and re-layouts  0.8 us (3%)
    pallas_call x1, Pallas kernels, shards(): pl.pallas_call(functools.partial(kernel, (R, A, C)), out_shape=pltpu.VMEM...  25.7 us
    unnamed x1, local copies, waits for them, and re-layouts  0.8 us

profile of v11, /device:TPU:0, one launch (start us, length us, event | category | flops | bytes accessed | tf_op | source)
XLA Modules:
  0.0 26.5 jit_solution(17092928613232071235)
XLA Ops:
  0.0 25.7 %shard_map.37 = bf16[256,1024]{1,0:T(8,128)(2,1)S(1)} custom-call(bf16[256,256]{1,0:T(8,128)(2,1)} %density_ref.1, bf16[256,2048]{1,0:T(8,128)(2,1)} %panel_ref.1, s32[2,2]{1,0:T(2,128)} %pattern_hbm.1), custom_call_target="tpu_custom_call" | custom-call | tf_op jit(solution)/shard_map/pallas_call | solution.py:287
  25.7 0.8 %copy.5 = bf16[256,1024]{1,0:T(8,128)(2,1)} copy(bf16[256,1024]{1,0:T(8,128)(2,1)S(1)} %shard_map.37) | data formatting | bytes 1048576

commit v12 on v10

--- a/solution.py
+++ b/solution.py
@@ -186,6 +186,26 @@
         for copy in own_piece(n):
             copy.start()
 
+    forwards = []
+
+    def forward(n):
+        known = len(sends)
+        qf, qs = first[n], second[n]
+        for dy in range(1, B):
+            arrived(piece(dy * A, qf), py_s.at[dy, qf], py_r.at[dy, qf], {"row": y_source(dy)})
+            for dx in range(1, A):
+                send(piece(dy * A + dx, qf), fx_s.at[dy, dx, qf], fx_r.at[dy, dx, qf],
+                     {"row": x_peer(dx)}, piece(dy * A, qf))
+        for dx in range(1, A):
+            arrived(piece(dx, qs), px_s.at[dx, qs], px_r.at[dx, qs], {"row": x_source(dx)})
+            for dy in range(1, B):
+                send(piece(dy * A + dx, qs), fy_s.at[dy, dx, qs], fy_r.at[dy, dx, qs],
+                     {"row": y_peer(dy)}, piece(dx, qs))
+        forwards.extend(sends[known:])
+        del sends[known:]
+
+    forward(0)
+
     for d in range(1, C):
         from_c = lax.rem(c - d + C, C)
         ref = frow.at[:, cols_of(from_c, l)]
@@ -222,19 +242,8 @@
             near.append((dy * A, dy * A + 1))
     far = [(dy * A + 1, dy * A + A) for dy in range(1, B)]
 
-    early = len(sends)
-    for qf, qs in zip(first, second):
-        for dy in range(1, B):
-            arrived(piece(dy * A, qf), py_s.at[dy, qf], py_r.at[dy, qf], {"row": y_source(dy)})
-            for dx in range(1, A):
-                send(piece(dy * A + dx, qf), fx_s.at[dy, dx, qf], fx_r.at[dy, dx, qf],
-                     {"row": x_peer(dx)}, piece(dy * A, qf))
-        for dx in range(1, A):
-            arrived(piece(dx, qs), px_s.at[dx, qs], px_r.at[dx, qs], {"row": x_source(dx)})
-            for dy in range(1, B):
-                send(piece(dy * A + dx, qs), fy_s.at[dy, dx, qs], fy_r.at[dy, dx, qs],
-                     {"row": y_peer(dy)}, piece(dx, qs))
-    late = len(sends)
+    for n in range(1, len(first)):
+        forward(n)
 
     for d in range(1, C):
         from_c = lax.rem(c - d + C, C)
@@ -254,7 +263,7 @@
     for q in range(PIECES):
         acc[:, part(q)] -= 2.0 * sum(by(grow, group, q) for group in near)
 
-    for copy in sends[:early] + sends[late:]:
+    for copy in sends:
         copy.wait_send()
     for qf, qs in zip(first, second):
         for dy in range(1, B):
@@ -268,7 +277,7 @@
                 total = total + (3.0 * by(frow, group, q) - 2.0 * by(grow, group, q))
             out_ref[:, part(q)] = total.astype(jnp.bfloat16)
 
-    for copy in sends[early:late]:
+    for copy in forwards:
         copy.wait_send()
 
 

time: 27 us -> 27 us (level)
  no operation moved by 1% of the time
where the time goes in v12:
time: 27 us; the launch traced here: 26.9 us
  Pallas kernels  26.1 us (97%)
  local copies, waits for them, and re-layouts  0.8 us (3%)
    pallas_call x1, Pallas kernels, shards(): pl.pallas_call(functools.partial(kernel, (R, A, C)), out_shape=pltpu.VMEM...  26.1 us
    unnamed x1, local copies, waits for them, and re-layouts  0.8 us

profile of v12, /device:TPU:1, one launch (start us, length us, event | category | flops | bytes accessed | tf_op | source)
XLA Modules:
  0.0 26.9 jit_solution(17018944712962423344)
XLA Ops:
  0.0 26.1 %shard_map.37 = bf16[256,1024]{1,0:T(8,128)(2,1)S(1)} custom-call(bf16[256,256]{1,0:T(8,128)(2,1)} %density_ref.1, bf16[256,2048]{1,0:T(8,128)(2,1)} %panel_ref.1, s32[2,2]{1,0:T(2,128)} %pattern_hbm.1), custom_call_target="tpu_custom_call" | custom-call | tf_op jit(solution)/shard_map/pallas_call | solution.py:296
  26.1 0.8 %copy.5 = bf16[256,1024]{1,0:T(8,128)(2,1)} copy(bf16[256,1024]{1,0:T(8,128)(2,1)S(1)} %shard_map.37) | data formatting | bytes 1048576

commit v13 on v12

--- a/solution.py
+++ b/solution.py
@@ -8,7 +8,7 @@
 from jax.sharding import PartitionSpec as P
 
 BS = 128
-PIECES = 4
+PIECES = 8
 MESH = pl.DeviceIdType.MESH
 
 
@@ -142,7 +142,7 @@
         prepare(fcol.at[rows_of(d * A), :], cy_s.at[d], cy_r.at[d], {"row": y_peer(d)}, own_rows)
         for d in range(1, B)
     ]
-    for n in range(2):
+    for n in range(PIECES // 2):
         over_row += own_piece(n)
     for copy in load_panel:
         copy.wait()
@@ -182,7 +182,7 @@
             send(half_rows(dy * A + dx, 1), ey_s.at[dy, dx], ey_r.at[dy, dx], {"row": y_peer(dy)},
                  half_rows(dx, 1))
 
-    for n in range(2, PIECES):
+    for n in range(PIECES // 2, PIECES):
         for copy in own_piece(n):
             copy.start()
 
@@ -204,7 +204,8 @@
         forwards.extend(sends[known:])
         del sends[known:]
 
-    forward(0)
+    for n in range(PIECES // 4):
+        forward(n)
 
     for d in range(1, C):
         from_c = lax.rem(c - d + C, C)
@@ -242,7 +243,7 @@
             near.append((dy * A, dy * A + 1))
     far = [(dy * A + 1, dy * A + A) for dy in range(1, B)]
 
-    for n in range(1, len(first)):
+    for n in range(PIECES // 4, len(first)):
         forward(n)
 
     for d in range(1, C):

time: 27 us -> 28.3 us (1.048)
  the two profiles are of different devices: /device:TPU:1 before, /device:TPU:0 now
where the time goes in v13:
time: 28.3 us; the launch traced here: 28 us
  Pallas kernels  27.2 us (96%)
  local copies, waits for them, and re-layouts  0.8 us (3%)
    pallas_call x1, Pallas kernels, shards(): pl.pallas_call(functools.partial(kernel, (R, A, C)), out_shape=pltpu.VMEM...  27.2 us
    unnamed x1, local copies, waits for them, and re-layouts  0.8 us

profile of v13, /device:TPU:0, one launch (start us, length us, event | category | flops | bytes accessed | tf_op | source)
XLA Modules:
  0.0 28.0 jit_solution(17311071447936446176)
XLA Ops:
  0.0 27.2 %shard_map.37 = bf16[256,1024]{1,0:T(8,128)(2,1)S(1)} custom-call(bf16[256,256]{1,0:T(8,128)(2,1)} %density_ref.1, bf16[256,2048]{1,0:T(8,128)(2,1)} %panel_ref.1, s32[2,2]{1,0:T(2,128)} %pattern_hbm.1), custom_call_target="tpu_custom_call" | custom-call | tf_op jit(solution)/shard_map/pallas_call | solution.py:297
  27.2 0.8 %copy.5 = bf16[256,1024]{1,0:T(8,128)(2,1)} copy(bf16[256,1024]{1,0:T(8,128)(2,1)S(1)} %shard_map.37) | data formatting | bytes 1048576
